TPU v7x, 32 devices: a whole 2x2x4 slice. The times are simulated.
32 devices in a mesh: lat: 4 (over y, x), lon: 8 (over z, core).
Axes of the slice: x: 2, y: 2, z: 4, core: 2. Of those that a mesh axis runs over, the one named last changes fastest.
Arguments:
- grid_feat: bfloat16 [64, 256, 1024], P('lat', 'lon'), may hold values from -40 to 40
- mesh_feat: bfloat16 [32, 128, 1024], P('lat', 'lon'), may hold values from -40 to 40
- edges: int32 [12, 64, 256], P(None, 'lat', 'lon'), may hold values from 0 to 4095, as said below
- edge_mask: int32 [12, 64, 256], P(None, 'lat', 'lon'), may hold values from 0 to 1, as said below
- w_query: bfloat16 [1024, 1024], replicated, may hold values from -0.1875 to 0.1875
- w_key: bfloat16 [1024, 1024], replicated, may hold values from -0.1875 to 0.1875
- w_value: bfloat16 [1024, 1024], replicated, may hold values from -0.1875 to 0.1875
- w_out: bfloat16 [1024, 1024], replicated, may hold values from -0.1875 to 0.1875
- cotangent: bfloat16 [64, 256, 1024], P('lat', 'lon'), may hold values from -6 to 6
Outputs:
- layer_out: bfloat16 [64, 256, 1024], P('lat', 'lon')
- grid_grad: bfloat16 [64, 256, 1024], P('lat', 'lon')
- mesh_grad: bfloat16 [32, 128, 1024], P('lat', 'lon')
Inputs may be any that keep to these rules, and one draw needn't show every extreme that they name: edges[e,i,j] = r * 128 + c names a mesh node with 0 <= r < 32, |r - i // 2| <= 4, and c within 4 of j // 2 around the circle of 128 columns; the 12 slots of a grid point name distinct nodes, masked slots included. `edge_mask`: each grid point has 3 to 12 live slots, and they come first.
All inputs are finite; a program needn't handle non-finite values.
Results may differ from a plain program's by a relative error of at most 0.01.
The roundings to bfloat16 on the way count: a program that leaves them out, or rounds other values in their place, can miss the bound.
Values may be sent and summed in bfloat16 or wider, within the bound.
A program may use at most 128 MiB of HBM per device.

v0:
```python
import math

import jax
import jax.numpy as jnp
from jax import lax
from jax.sharding import PartitionSpec as P

HEAD_COUNT = 16
EDGE_SLOTS = 12
HALO_REACH = 4


NEG_FILL = -1e30


def padded_2(block, sides, width, periodic):
    for axis, dim in sides:
        count = lax.axis_size(axis)
        forward = [(i, i + 1) for i in range(count - 1)]
        if periodic:
            forward.append((count - 1, 0))
        backward = [(target, source) for source, target in forward]
        low = lax.ppermute(
            lax.slice_in_dim(block, block.shape[dim] - width, None, axis=dim), axis, forward
        )
        high = lax.ppermute(lax.slice_in_dim(block, 0, width, axis=dim), axis, backward)
        block = jnp.concatenate([low, block, high], axis=dim)
    return block


def fetch_tile(tile):
    return padded_2(tile, (("lat", 0), ("lon", 1)), HALO_REACH, True)


def send_rims_back(padded):
    cols_inner = padded.shape[1] - 2 * HALO_REACH
    rows_inner = padded.shape[0] - 2 * HALO_REACH
    lon_rims = jnp.concatenate([padded[:, :HALO_REACH], padded[:, -HALO_REACH:]], axis=1)
    lon_back = padded_2(lon_rims, (("lon", 1),), HALO_REACH, True)
    middle = padded[:, HALO_REACH : HALO_REACH + cols_inner]
    middle = middle + jnp.pad(
        lon_back[:, :HALO_REACH], ((0, 0), (0, cols_inner - HALO_REACH), (0, 0))
    )
    middle = middle + jnp.pad(
        lon_back[:, 3 * HALO_REACH :], ((0, 0), (cols_inner - HALO_REACH, 0), (0, 0))
    )
    lat_rims = jnp.concatenate([middle[:HALO_REACH], middle[-HALO_REACH:]], axis=0)
    lat_back = padded_2(lat_rims.astype(jnp.bfloat16), (("lat", 0),), HALO_REACH, False).astype(
        lat_rims.dtype
    )
    owned = middle[HALO_REACH : HALO_REACH + rows_inner]
    owned = owned + jnp.pad(lat_back[:HALO_REACH], ((0, rows_inner - HALO_REACH), (0, 0), (0, 0)))
    owned = owned + jnp.pad(
        lat_back[3 * HALO_REACH :], ((rows_inner - HALO_REACH, 0), (0, 0), (0, 0))
    )
    return owned


def local(grid_feat, mesh_feat, edges, edge_mask, w_query, w_key, w_value, w_out, cotangent):
    grid_rows, grid_cols, width = grid_feat.shape
    mesh_rows, mesh_cols = (mesh_feat.shape[0], mesh_feat.shape[1])
    points = grid_rows * grid_cols
    head_size = width // HEAD_COUNT
    score_scale = 1.0 / math.sqrt(head_size)
    padded_rows = mesh_rows + 2 * HALO_REACH
    padded_cols = mesh_cols + 2 * HALO_REACH
    padded_count = padded_rows * padded_cols
    lon_total = mesh_cols * lax.axis_size("lon")
    w_pair = jnp.concatenate([w_key, w_value], axis=1)
    padded_feat = fetch_tile(mesh_feat).reshape(padded_count, width)
    padded_pair = jnp.dot(padded_feat, w_pair, preferred_element_type=jnp.float32).astype(
        jnp.bfloat16
    )
    key_rows = padded_pair[:, :width].reshape(padded_count, HEAD_COUNT, head_size)
    value_rows = padded_pair[:, width:].reshape(padded_count, HEAD_COUNT, head_size)
    lat_start = lax.axis_index("lat") * mesh_rows
    lon_start = lax.axis_index("lon") * mesh_cols
    targets = edges.reshape(EDGE_SLOTS, points)
    live = edge_mask.reshape(EDGE_SLOTS, points)
    target_lat = targets // lon_total - lat_start + HALO_REACH
    target_lon = jnp.mod(targets % lon_total - lon_start + HALO_REACH, lon_total)
    local_slot = target_lat * padded_cols + target_lon
    candidates = lax.broadcasted_iota(jnp.int32, (1, 1, padded_count), 2)
    linked = jnp.sum(
        jnp.where((local_slot[:, :, None] == candidates) & (live[:, :, None] > 0), 1, 0), axis=0
    )
    allowed = linked > 0
    grid_flat = grid_feat.reshape(points, width)
    queries = jnp.dot(grid_flat, w_query, preferred_element_type=jnp.float32).astype(jnp.bfloat16)
    query_heads = queries.reshape(points, HEAD_COUNT, head_size)
    scores = (
        jnp.einsum("rhd,phd->hrp", query_heads, key_rows, preferred_element_type=jnp.float32)
        * score_scale
    )
    scores = jnp.where(allowed[None], scores, NEG_FILL)
    row_max = jnp.max(scores, axis=2, keepdims=True)
    exp_scores = jnp.exp(scores - row_max)
    prob_full = exp_scores / jnp.sum(exp_scores, axis=2, keepdims=True)
    probs_half = prob_full.astype(jnp.bfloat16)
    attended = jnp.einsum(
        "hrp,phd->rhd", probs_half, value_rows, preferred_element_type=jnp.float32
    )
    attended = attended.astype(jnp.bfloat16).reshape(points, width)
    layer_out = (
        grid_flat.astype(jnp.float32) + jnp.dot(attended, w_out, preferred_element_type=jnp.float32)
    ).astype(jnp.bfloat16)
    cot_rows = cotangent.reshape(points, width)
    d_attended = jnp.dot(cot_rows, w_out.T, preferred_element_type=jnp.float32).astype(jnp.bfloat16)
    d_heads = d_attended.reshape(points, HEAD_COUNT, head_size)
    d_probs = jnp.einsum("rhd,phd->hrp", d_heads, value_rows, preferred_element_type=jnp.float32)
    centred = jnp.sum(prob_full * d_probs, axis=2, keepdims=True)
    d_scores = (prob_full * (d_probs - centred) * score_scale).astype(jnp.bfloat16)
    d_query = jnp.einsum("hrp,phd->rhd", d_scores, key_rows, preferred_element_type=jnp.float32)
    d_query = d_query.astype(jnp.bfloat16).reshape(points, width)
    grid_grad = (
        cot_rows.astype(jnp.float32)
        + jnp.dot(d_query, w_query.T, preferred_element_type=jnp.float32)
    ).astype(jnp.bfloat16)
    d_keys = jnp.einsum(
        "hrp,rhd->phd", d_scores, query_heads, preferred_element_type=jnp.float32
    ).reshape(padded_count, width)
    d_values = jnp.einsum(
        "hrp,rhd->phd", probs_half, d_heads, preferred_element_type=jnp.float32
    ).reshape(padded_count, width)
    d_pair = jnp.concatenate([d_keys, d_values], axis=1)
    owned = send_rims_back(d_pair.reshape(padded_rows, padded_cols, 2 * width)).reshape(
        mesh_rows * mesh_cols, 2 * width
    )
    owned_half = owned.astype(jnp.bfloat16)
    mesh_grad = jnp.dot(owned_half, w_pair.T, preferred_element_type=jnp.float32).astype(
        jnp.bfloat16
    )
    return (
        layer_out.reshape(grid_rows, grid_cols, width),
        grid_grad.reshape(grid_rows, grid_cols, width),
        mesh_grad.reshape(mesh_rows, mesh_cols, width),
    )


def solution(mesh):
    placed = (
        P("lat", "lon", None),
        P("lat", "lon", None),
        P(None, "lat", "lon"),
        P(None, "lat", "lon"),
        P(),
        P(),
        P(),
        P(),
        P("lat", "lon", None),
    )
    return jax.shard_map(
        local,
        mesh=mesh,
        in_specs=placed,
        out_specs=(P("lat", "lon", None), P("lat", "lon", None), P("lat", "lon", None)),
        check_vma=False,
    )
```

profile of v0, /device:TPU:4, one launch (start us, length us, event | category | flops | bytes accessed | tf_op | source)
XLA Modules:
  0.0 155.0 jit_solution(13475066178263541888)
XLA Ops:
  0.6 0.0 copy-start
  0.6 1.8 %fusion.59 = (bf16[4,16,1024]{2,1,0:T(8,128)(2,1)}, bf16[4,16,1024]{2,1,0:T(8,128)(2,1)}) fusion(bf16[8,16,1024]{2,1,0:T(8,128)(2,1)} %param.10), kind=kLoop, calls=%fused_computation.79 | loop fusion | bytes 524288 | tf_op jit(solution)/shard_map/slice | solution.py:26
  2.5 1.5 collective-permute-start
  4.0 1.4 collective-permute-start.1
  5.4 1.0 reshape.137
  6.4 0.9 broadcast_compare_fusion.1
  7.3 0.1 gt.23
  7.4 0.1 fusion.41
  7.5 2.6 %select_reduce_fusion = s32[512,384]{1,0:T(8,128)S(1)} fusion(s32[12,512]{1,0:T(8,128)S(1)} %fusion.41, pred[12,512]{1,0:T(8,128)(4,1)S(1)} %gt.23), kind=kLoop, calls=%fused_computation.8 | loop fusion | flops 9240576 | bytes 817152 | tf_op jit(solution)/shard_map/reduce_sum | solution.py:84
  10.1 0.1 broadcast_compare_fusion
  10.2 1.0 copy.35
  11.1 3.2 %convolution_convert_fusion.2 = bf16[512,1024]{1,0:T(8,128)(2,1)S(1)} fusion(bf16[512,1024]{1,0:T(8,128)(2,1)} %bitcast.54, bf16[1024,1024]{1,0:T(8,128)(2,1)} %param.13), kind=kOutput, calls=%fused_computation.30 | convolution fusion | flops 1074266112 | bytes 4194304 | tf_op jit(solution)/shard_map/dot_general | solution.py:89
  14.3 1.3 copy.36
  15.6 0.0 copy-done
  15.7 3.5 %convolution_convert_fusion.1 = bf16[512,1024]{1,0:T(8,128)(2,1)} fusion(bf16[512,1024]{1,0:T(8,128)(2,1)} %bitcast.56, bf16[1024,1024]{1,0:T(8,128)(2,1)S(1)} %copy-done), kind=kOutput, calls=%fused_computation.29 | convolution fusion | flops 1074266112 | bytes 4194304 | tf_op jit(solution)/shard_map/dot_general | solution.py:108
  19.1 1.5 copy.39
  20.7 0.0 copy-start.4
  20.7 1.9 %constant_dynamic-update-slice_fusion.4 = bf16[1024,2048]{1,0:T(8,128)(2,1)S(1)} fusion(bf16[1024,1024]{1,0:T(8,128)(2,1)} %param.14), kind=kLoop, calls=%fused_computation.65 | loop fusion | bytes 4194304
  22.6 0.0 collective-permute-done
  22.6 0.9 constant_dynamic-update-slice_fusion.2
  23.5 0.0 copy-done.5
  23.6 0.0 collective-permute-done.1
  23.6 0.1 fusion.58
  23.7 2.5 %collective-permute-start.3 = (bf16[16,4,1024]{2,1,0:T(4,128)(2,1)S(1)}, bf16[16,4,1024]{2,1,0:T(4,128)(2,1)S(1)}, u32[]{:S(2)}, u32[]{:S(2)}) collective-permute-start(bf16[16,4,1024]{2,1,0:T(4,128)(2,1)S(1)} %get-tuple-element.12), channel_id=1, source_target_pairs={{1,0},{2,1},{3,2},{4,3},{5,4},{6,5},{7,6},{0,7},{9,8},{10,9},{11,1... | collective-permute-start | bytes 393224 | tf_op jit(solution)/shard_map/ppermute | solution.py:26
  26.2 0.0 collective-permute-start.2
  26.2 0.0 copy-done.4
  26.3 0.2 constant_dynamic-update-slice_fusion.3
  26.5 0.0 copy-start.1
  26.5 2.4 %collective-permute-done.3 = bf16[16,4,1024]{2,1,0:T(4,128)(2,1)S(1)} collective-permute-done((bf16[16,4,1024]{2,1,0:T(4,128)(2,1)S(1)}, bf16[16,4,1024]{2,1,0:T(4,128)(2,1)S(1)}, u32[]{:S(2)}, u32[]{:S(2)}) %collective-permute-start.3) | collective-permute-done | bytes 131104 | tf_op jit(solution)/shard_map/ppermute | solution.py:26
  29.0 3.5 %collective-permute-done.2 = bf16[16,4,1024]{2,1,0:T(4,128)(2,1)S(1)} collective-permute-done((bf16[16,4,1024]{2,1,0:T(4,128)(2,1)S(1)}, bf16[16,4,1024]{2,1,0:T(4,128)(2,1)S(1)}, u32[]{:S(2)}, u32[]{:S(2)}) %collective-permute-start.2) | collective-permute-done | bytes 131104 | tf_op jit(solution)/shard_map/ppermute | solution.py:23
  32.4 0.4 pad_maximum_fusion
  32.8 1.8 %convolution_convert_fusion = bf16[384,2048]{1,0:T(8,128)(2,1)S(1)} fusion(bf16[384,1024]{1,0:T(8,128)(2,1)S(1)} %bitcast.52, bf16[1024,2048]{1,0:T(8,128)(2,1)S(1)} %constant_dynamic-update-slice_fusion.3), kind=kOutput, calls=%fused_computation.21 | convolution fusion | flops 1611399168 | bytes 6553600 | tf_op jit(solution)/shard_map/dot_general | solution.py:71
  34.7 0.0 copy-done.1
  34.7 1.3 fusion.56
  36.0 2.4 %copy.34 = bf16[384,1024]{0,1:T(8,128)(2,1)} copy(bf16[384,1024]{1,0:T(8,128)(2,1)} %get-tuple-element.8) | data formatting | bytes 1572864 | tf_op jit(solution)/shard_map/slice | solution.py:75
  38.3 2.3 %copy.37 = bf16[384,1024]{0,1:T(8,128)(2,1)} copy(bf16[384,1024]{1,0:T(8,128)(2,1)} %get-tuple-element.7) | data formatting | bytes 1572864 | tf_op jit(solution)/shard_map/slice | solution.py:74
  40.6 7.5 %fusion.61 = f32[16,512,384]{1,2,0:T(8,128)} fusion(bf16[512,16,64]{0,2,1:T(8,128)(2,1)S(1)} %bitcast.43, bf16[384,16,64]{0,2,1:T(8,128)(2,1)} %bitcast.45), kind=kOutput, calls=%fused_computation.81 | convolution fusion | flops 402653184 | bytes 14417920 | tf_op jit(solution)/shard_map/rhd,phd->hrp/dot_general | solution.py:110
  48.1 10.7 %fusion.60 = (f32[16,512]{1,0:T(8,128)S(1)}, f32[16,512,384]{1,2,0:T(8,128)}) fusion(pred[512,384]{0,1:T(8,128)(4,1)S(1)} %copy-done.7, bf16[512,16,64]{0,2,1:T(8,128)(2,1)} %bitcast.48, bf16[384,16,64]{0,2,1:T(8,128)(2,1)} %bitcast.50), kind=kOutput, calls=%fused_computation.80 | convolution fusion | flops 415236480 | bytes 14647296 | tf_op jit(solution)/shard_map/sub | solution.py:97
  58.8 7.2 %fusion.21 = bf16[16,64,512]{2,1,0:T(8,128)(2,1)} fusion(bf16[384,16,64]{0,2,1:T(8,128)(2,1)} %bitcast.46, f32[16,512,384]{1,2,0:T(8,128)} %get-tuple-element.16, f32[16,512]{1,0:T(8,128)S(1)} %get-tuple-element.15), kind=kOutput, calls=%fused_computation.26 | convolution fusion | flops 409468928 | bytes 14450688 | tf_op jit(solution)/shard_map/hrp,phd->rhd/dot_general | solution.py:100
  66.0 1.6 %copy-done.12 = f32[16,512,384]{1,2,0:T(8,128)S(1)} copy-done((f32[16,512,384]{1,2,0:T(8,128)S(1)}, f32[16,512,384]{1,2,0:T(8,128)}, u32[]{:S(2)}) %copy-start.12) | copy-done | bytes 12582936
  67.6 3.3 %fusion.24 = f32[384,16,64]{0,2,1:T(8,128)} fusion(bf16[512,16,64]{0,2,1:T(8,128)(2,1)S(1)} %bitcast.44, f32[16,512,384]{1,2,0:T(8,128)S(1)} %copy-done.12, f32[16,512]{1,0:T(8,128)S(1)} %get-tuple-element.15), kind=kOutput, calls=%fused_computation.27 | convolution fusion | flops 408944640 | bytes 15237120 | tf_op jit(solution)/shard_map/hrp,rhd->phd/dot_general | solution.py:122
  70.8 18.7 %fusion.30 = f32[384,16,64]{0,2,1:T(8,128)} fusion(bf16[512,16,64]{0,2,1:T(8,128)(2,1)} %bitcast.49, f32[16,512,384]{1,2,0:T(8,128)} %fusion.61, f32[16,512,384]{1,2,0:T(8,128)} %get-tuple-element.16, f32[16,512]{1,0:T(8,128)S(1)} %get-tuple-element.15), kind=kOutput, calls=%fused_computation.31 | convolution fusion | flops 424681856 | bytes 27820032 | tf_op jit(solution)/shard_map/hrp,rhd->phd/dot_general | solution.py:119
  89.6 3.3 %copy.42 = f32[384,16,64]{2,1,0:T(8,128)} copy(f32[384,16,64]{0,2,1:T(8,128)} %fusion.30) | data formatting | bytes 3145728 | tf_op jit(solution)/shard_map/hrp,rhd->phd/transpose | solution.py:119
  92.8 3.7 %concatenate.26 = f32[16,24,1024]{2,1,0:T(8,128)} reshape(f32[384,16,64]{2,1,0:T(8,128)} %copy.42) | data formatting | bytes 3145728 | tf_op jit(solution)/shard_map/concatenate | solution.py:125
  96.5 2.7 %constant_dynamic-update-slice_fusion.6 = f32[16,24,2048]{2,1,0:T(8,128)} fusion(f32[16,24,1024]{2,1,0:T(8,128)} %concatenate.26), kind=kLoop, calls=%fused_computation.67 | loop fusion | bytes 3145728
  99.3 3.3 %copy.44 = f32[384,16,64]{2,1,0:T(8,128)} copy(f32[384,16,64]{0,2,1:T(8,128)} %fusion.24) | data formatting | bytes 3145728 | tf_op jit(solution)/shard_map/hrp,rhd->phd/transpose | solution.py:122
  102.6 3.8 %concatenate.27 = f32[16,24,1024]{2,1,0:T(8,128)} reshape(f32[384,16,64]{2,1,0:T(8,128)} %copy.44) | data formatting | bytes 3145728 | tf_op jit(solution)/shard_map/concatenate | solution.py:125
  106.4 2.7 %constant_dynamic-update-slice_fusion.5 = f32[16,24,2048]{2,1,0:T(8,128)} fusion(f32[16,24,2048]{2,1,0:T(8,128)} %constant_dynamic-update-slice_fusion.6, f32[16,24,1024]{2,1,0:T(8,128)} %concatenate.27), kind=kLoop, calls=%fused_computation.66 | loop fusion | bytes 3145728 | tf_op jit(solution)/shard_map/concatenate | solution.py:125
  109.1 2.8 %fusion.55 = (f32[16,4,2048]{2,1,0:T(4,128)}, f32[16,4,2048]{2,1,0:T(4,128)}) fusion(f32[16,24,2048]{2,1,0:T(8,128)} %constant_dynamic-update-slice_fusion.5), kind=kLoop, calls=%fused_computation.75 | loop fusion | bytes 2097152 | tf_op jit(solution)/shard_map/slice | solution.py:38
  111.9 0.3 collective-permute-start.5
  112.2 0.2 collective-permute-start.4
  112.4 18.4 %fusion.27 = bf16[16,64,512]{2,1,0:T(8,128)(2,1)} fusion(bf16[384,16,64]{0,2,1:T(8,128)(2,1)S(1)} %bitcast.51, f32[16,512,384]{1,2,0:T(8,128)} %fusion.61, f32[16,512,384]{1,2,0:T(8,128)} %get-tuple-element.16, f32[16,512]{1,0:T(8,128)S(1)} %get-tuple-element.15), kind=kOutput, calls=%fused_computation.28 | convolution fusion | flops 425206144 | bytes 27033600 | tf_op jit(solution)/shard_map/hrp,phd->rhd/dot_general | solution.py:113
  130.8 3.9 %add_convert_fusion.1 = bf16[512,1024]{1,0:T(8,128)(2,1)} fusion(bf16[512,1024]{1,0:T(8,128)(2,1)} %bitcast.55, bf16[512,1024]{0,1:T(8,128)(2,1)} %bitcast.59, bf16[1024,1024]{1,0:T(8,128)(2,1)S(1)} %copy-done), kind=kOutput, calls=%fused_computation.25 | convolution fusion | flops 1075314688 | bytes 5242880 | tf_op jit(solution)/shard_map/dot_general | solution.py:105
  134.7 0.0 collective-permute-done.5
  134.7 0.0 collective-permute-done.4
  134.7 1.8 %fusion.53 = (bf16[16,16,2048]{2,1,0:T(8,128)(2,1)S(1)}, f32[16,16,2048]{2,1,0:T(8,128)S(1)}) fusion(f32[16,4,2048]{2,1,0:T(4,128)S(1)} %collective-permute-done.5, f32[16,4,2048]{2,1,0:T(4,128)} %collective-permute-done.4, f32[16,24,2048]{2,1,0:T(8,128)S(1)} %copy-done.3), kind=kLoop, calls=%fused_computation.74 | loop fusion | flops 1572864 | bytes 6291456 | tf_op jit(solution)/shard_map/convert.2
  136.6 2.4 %collective-permute-start.7 = (bf16[4,16,2048]{2,1,0:T(8,128)(2,1)S(1)}, bf16[4,16,2048]{2,1,0:T(8,128)(2,1)S(1)}, u32[]{:S(2)}, u32[]{:S(2)}) collective-permute-start(bf16[4,16,2048]{2,1,0:T(8,128)(2,1)S(1)} %get-tuple-element.10), channel_id=1, source_target_pairs={{8,0},{16,8},{24,16},{9,1},{17,9},{25,17},{10,2},{18,10},{26,18},{... | collective-permute-start | bytes 786440 | tf_op jit(solution)/shard_map/ppermute | solution.py:26
  139.1 3.4 %collective-permute-start.6 = (bf16[4,16,2048]{2,1,0:T(8,128)(2,1)S(1)}, bf16[4,16,2048]{2,1,0:T(8,128)(2,1)S(1)}, u32[]{:S(2)}, u32[]{:S(2)}) collective-permute-start(bf16[4,16,2048]{2,1,0:T(8,128)(2,1)S(1)} %get-tuple-element.9), channel_id=1, source_target_pairs={{0,8},{8,16},{16,24},{1,9},{9,17},{17,25},{2,10},{10,18},{18,26},{... | collective-permute-start | bytes 786440 | tf_op jit(solution)/shard_map/ppermute | solution.py:23
  142.5 2.3 %add_convert_fusion = bf16[512,1024]{1,0:T(8,128)(2,1)} fusion(bf16[512,1024]{1,0:T(8,128)(2,1)S(1)} %bitcast.57, bf16[512,1024]{0,1:T(8,128)(2,1)S(1)} %bitcast.60, bf16[1024,1024]{1,0:T(8,128)(2,1)S(1)} %copy-done.9), kind=kOutput, calls=%fused_computation.24 | convolution fusion | flops 1075314688 | bytes 5242880 | tf_op jit(solution)/shard_map/dot_general | solution.py:117
  144.8 1.9 %collective-permute-done.7 = bf16[4,16,2048]{2,1,0:T(8,128)(2,1)S(1)} collective-permute-done((bf16[4,16,2048]{2,1,0:T(8,128)(2,1)S(1)}, bf16[4,16,2048]{2,1,0:T(8,128)(2,1)S(1)}, u32[]{:S(2)}, u32[]{:S(2)}) %collective-permute-start.7) | collective-permute-done | bytes 262176 | tf_op jit(solution)/shard_map/ppermute | solution.py:26
  146.7 5.6 %collective-permute-done.6 = bf16[4,16,2048]{2,1,0:T(8,128)(2,1)S(1)} collective-permute-done((bf16[4,16,2048]{2,1,0:T(8,128)(2,1)S(1)}, bf16[4,16,2048]{2,1,0:T(8,128)(2,1)S(1)}, u32[]{:S(2)}, u32[]{:S(2)}) %collective-permute-start.6) | collective-permute-done | bytes 262176 | tf_op jit(solution)/shard_map/ppermute | solution.py:23
  152.3 0.2 maximum_convert_fusion
  152.5 0.2 fusion.37
  152.8 2.2 %convolution_convert_fusion.3 = bf16[128,1024]{1,0:T(8,128)(2,1)} fusion(bf16[128,2048]{1,0:T(8,128)(2,1)S(1)} %bitcast.47, bf16[1024,2048]{1,0:T(8,128)(2,1)S(1)} %copy-done.2), kind=kOutput, calls=%fused_computation.33 | convolution fusion | flops 537001984 | bytes 4980736 | tf_op jit(solution)/shard_map/dot_general | solution.py:130
  (22 shorter events, 0.1 us)
Async XLA Ops:
  0.6 15.0 %copy-start = (bf16[1024,1024]{1,0:T(8,128)(2,1)S(1)}, bf16[1024,1024]{1,0:T(8,128)(2,1)}, u32[]{:S(2)}) copy-start(bf16[1024,1024]{1,0:T(8,128)(2,1)} %param.16) | copy-start | bytes 6291460
  2.5 20.1 %collective-permute-start = (bf16[4,16,1024]{2,1,0:T(8,128)(2,1)}, bf16[4,16,1024]{2,1,0:T(8,128)(2,1)}, u32[]{:S(2)}, u32[]{:S(2)}) collective-permute-start(bf16[4,16,1024]{2,1,0:T(8,128)(2,1)} %get-tuple-element.14), channel_id=1, source_target_pairs={{0,8},{8,16},{16,24},{24,0},{1,9},{9,17},{17,25},{25,1},{2,10},{10... | collective-permute-start | bytes 393224 | tf_op jit(solution)/shard_map/ppermute | solution.py:23
  4.0 19.6 %collective-permute-start.1 = (bf16[4,16,1024]{2,1,0:T(8,128)(2,1)}, bf16[4,16,1024]{2,1,0:T(8,128)(2,1)S(1)}, u32[]{:S(2)}, u32[]{:S(2)}) collective-permute-start(bf16[4,16,1024]{2,1,0:T(8,128)(2,1)} %get-tuple-element.13), channel_id=1, source_target_pairs={{8,0},{16,8},{24,16},{0,24},{9,1},{17,9},{25,17},{1,25},{10,2},{18... | collective-permute-start | bytes 393224 | tf_op jit(solution)/shard_map/ppermute | solution.py:26
  19.1 4.4 %copy-start.5 = (bf16[8,16,1024]{2,1,0:T(8,128)(2,1)S(1)}, bf16[8,16,1024]{2,1,0:T(8,128)(2,1)}, u32[]{:S(2)}) copy-start(bf16[8,16,1024]{2,1,0:T(8,128)(2,1)} %param.10) | copy-start | bytes 786436
  20.7 5.6 %copy-start.4 = (bf16[1024,1024]{1,0:T(8,128)(2,1)S(1)}, bf16[1024,1024]{1,0:T(8,128)(2,1)}, u32[]{:S(2)}) copy-start(bf16[1024,1024]{1,0:T(8,128)(2,1)} %param.15) | copy-start | bytes 6291460
  23.7 5.2 %collective-permute-start.3 = (bf16[16,4,1024]{2,1,0:T(4,128)(2,1)S(1)}, bf16[16,4,1024]{2,1,0:T(4,128)(2,1)S(1)}, u32[]{:S(2)}, u32[]{:S(2)}) collective-permute-start(bf16[16,4,1024]{2,1,0:T(4,128)(2,1)S(1)} %get-tuple-element.12), channel_id=1, source_target_pairs={{1,0},{2,1},{3,2},{4,3},{5,4},{6,5},{7,6},{0,7},{9,8},{10,9},{11,1... | collective-permute-start | bytes 393224 | tf_op jit(solution)/shard_map/ppermute | solution.py:26
  26.2 6.2 %collective-permute-start.2 = (bf16[16,4,1024]{2,1,0:T(4,128)(2,1)S(1)}, bf16[16,4,1024]{2,1,0:T(4,128)(2,1)S(1)}, u32[]{:S(2)}, u32[]{:S(2)}) collective-permute-start(bf16[16,4,1024]{2,1,0:T(4,128)(2,1)S(1)} %get-tuple-element.11), channel_id=1, source_target_pairs={{0,1},{1,2},{2,3},{3,4},{4,5},{5,6},{6,7},{7,0},{8,9},{9,10},{10,1... | collective-permute-start | bytes 393224 | tf_op jit(solution)/shard_map/ppermute | solution.py:23
  26.5 8.2 %copy-start.1 = (bf16[1024,2048]{1,0:T(8,128)(2,1)}, bf16[1024,2048]{1,0:T(8,128)(2,1)S(1)}, u32[]{:S(2)}) copy-start(bf16[1024,2048]{1,0:T(8,128)(2,1)S(1)} %constant_dynamic-update-slice_fusion.3) | copy-start | bytes 12582916
  40.6 7.5 %copy-start.7 = (pred[512,384]{0,1:T(8,128)(4,1)S(1)}, pred[512,384]{0,1:T(8,128)(4,1)}, u32[]{:S(2)}) copy-start(pred[512,384]{0,1:T(8,128)(4,1)} %copy.35) | copy-start | bytes 589828
  58.8 8.8 %copy-start.12 = (f32[16,512,384]{1,2,0:T(8,128)S(1)}, f32[16,512,384]{1,2,0:T(8,128)}, u32[]{:S(2)}) copy-start(f32[16,512,384]{1,2,0:T(8,128)} %get-tuple-element.16) | copy-start | bytes 37748740
  102.6 9.8 %copy-start.6 = (bf16[384,1024]{0,1:T(8,128)(2,1)S(1)}, bf16[384,1024]{0,1:T(8,128)(2,1)}, u32[]{:S(2)}) copy-start(bf16[384,1024]{0,1:T(8,128)(2,1)} %copy.37) | copy-start | bytes 2359300
  111.9 22.9 %collective-permute-start.5 = (f32[16,4,2048]{2,1,0:T(4,128)}, f32[16,4,2048]{2,1,0:T(4,128)S(1)}, u32[]{:S(2)}, u32[]{:S(2)}) collective-permute-start(f32[16,4,2048]{2,1,0:T(4,128)} %get-tuple-element.6), channel_id=1, source_target_pairs={{1,0},{2,1},{3,2},{4,3},{5,4},{6,5},{7,6},{0,7},{9,8},{10,9},{11,1... | collective-permute-start | bytes 1572872 | tf_op jit(solution)/shard_map/ppermute | solution.py:26
  112.2 22.5 %collective-permute-start.4 = (f32[16,4,2048]{2,1,0:T(4,128)}, f32[16,4,2048]{2,1,0:T(4,128)}, u32[]{:S(2)}, u32[]{:S(2)}) collective-permute-start(f32[16,4,2048]{2,1,0:T(4,128)} %get-tuple-element.5), channel_id=1, source_target_pairs={{0,1},{1,2},{2,3},{3,4},{4,5},{5,6},{6,7},{7,0},{8,9},{9,10},{10,1... | collective-permute-start | bytes 1572872 | tf_op jit(solution)/shard_map/ppermute | solution.py:23
  130.8 4.0 %copy-start.3 = (f32[16,24,2048]{2,1,0:T(8,128)S(1)}, f32[16,24,2048]{2,1,0:T(8,128)}, u32[]{:S(2)}) copy-start(f32[16,24,2048]{2,1,0:T(8,128)} %constant_dynamic-update-slice_fusion.5) | copy-start | bytes 9437188
  134.7 7.8 %copy-start.9 = (bf16[1024,1024]{1,0:T(8,128)(2,1)S(1)}, bf16[1024,1024]{1,0:T(8,128)(2,1)}, u32[]{:S(2)}) copy-start(bf16[1024,1024]{1,0:T(8,128)(2,1)} %param.13) | copy-start | bytes 6291460
  134.7 7.8 %copy-start.10 = (bf16[16,32,1024]{2,1,0:T(8,128)(2,1)S(1)}, bf16[16,32,1024]{2,1,0:T(8,128)(2,1)}, u32[]{:S(2)}) copy-start(bf16[16,32,1024]{2,1,0:T(8,128)(2,1)} %param.17) | copy-start | bytes 3145732
  134.7 7.8 %copy-start.11 = (bf16[16,64,512]{2,1,0:T(8,128)(2,1)S(1)}, bf16[16,64,512]{2,1,0:T(8,128)(2,1)}, u32[]{:S(2)}) copy-start(bf16[16,64,512]{2,1,0:T(8,128)(2,1)} %fusion.27) | copy-start | bytes 3145732
  136.6 10.1 %collective-permute-start.7 = (bf16[4,16,2048]{2,1,0:T(8,128)(2,1)S(1)}, bf16[4,16,2048]{2,1,0:T(8,128)(2,1)S(1)}, u32[]{:S(2)}, u32[]{:S(2)}) collective-permute-start(bf16[4,16,2048]{2,1,0:T(8,128)(2,1)S(1)} %get-tuple-element.10), channel_id=1, source_target_pairs={{8,0},{16,8},{24,16},{9,1},{17,9},{25,17},{10,2},{18,10},{26,18},{... | collective-permute-start | bytes 786440 | tf_op jit(solution)/shard_map/ppermute | solution.py:26
  139.1 13.2 %collective-permute-start.6 = (bf16[4,16,2048]{2,1,0:T(8,128)(2,1)S(1)}, bf16[4,16,2048]{2,1,0:T(8,128)(2,1)S(1)}, u32[]{:S(2)}, u32[]{:S(2)}) collective-permute-start(bf16[4,16,2048]{2,1,0:T(8,128)(2,1)S(1)} %get-tuple-element.9), channel_id=1, source_target_pairs={{0,8},{8,16},{16,24},{1,9},{9,17},{17,25},{2,10},{10,18},{18,26},{... | collective-permute-start | bytes 786440 | tf_op jit(solution)/shard_map/ppermute | solution.py:23
  144.8 7.7 %copy-start.8 = (pred[8]{0:T(512)(128)(4,1)S(1)}, pred[8]{0:T(512)(128)(4,1)}, u32[]{:S(2)}) copy-start(pred[8]{0:T(512)(128)(4,1)} %constant.63.clone.1) | copy-start | bytes 28
  144.8 8.0 %copy-start.2 = (bf16[1024,2048]{1,0:T(8,128)(2,1)S(1)}, bf16[1024,2048]{1,0:T(8,128)(2,1)}, u32[]{:S(2)}) copy-start(bf16[1024,2048]{1,0:T(8,128)(2,1)} %copy-done.1) | copy-start | bytes 12582916
where the time goes:
time: 156 us; the launch traced here: 155 us
  matrix products  82.6 us (53%)
  local copies, waits for them, and re-layouts  39.9 us (26%)
  waiting for transfers between devices  13.5 us (9%)
  starting transfers between devices  11.8 us (8%)
  other arithmetic  6.3 us (4%)
    dot_general x1, matrix products, local(): jnp.einsum('hrp,rhd->phd', d_scores, query_heads, preferred_element_type=...  18.7 us
    dot_general x1, matrix products, local(): jnp.einsum('hrp,phd->rhd', d_scores, key_rows, preferred_element_type=jnp...  18.4 us
    sub x1, matrix products, local(): exp_scores = jnp.exp(scores - row_max)  10.7 us
    concatenate x3, local copies, waits for them, and re-layouts, local(): d_pair = jnp.concatenate([d_keys, d_values], axis=1)  10.2 us
    ppermute x4, waiting for transfers between devices, padded_2(): lax.ppermute(lax.slice_in_dim(block, block.shape[dim] - width, None, axis...  9.06 us
    dot_general x1, matrix products, local(): jnp.einsum('rhd,phd->hrp', d_heads, value_rows, preferred_element_type=jn...  7.48 us
    unnamed x30, local copies, waits for them, and re-layouts  7.22 us
    dot_general x1, matrix products, local(): jnp.einsum('hrp,phd->rhd', probs_half, value_rows, preferred_element_type...  7.18 us
  transfers between devices with their start and end apart: 8, of which 4 were waited for; matrix products, arithmetic and copies ran while one was open for 28% of the time, Pallas kernels for 0%

commit v1 on v0

v1 whole, which is shorter than its diff:
```python
import functools
import math

import jax
import jax.numpy as jnp
from jax import lax
from jax.experimental import pallas as pl
from jax.experimental.pallas import tpu as pltpu
from jax.sharding import PartitionSpec as P

HEAD_COUNT = 16
EDGE_SLOTS = 12
HALO_REACH = 4
TILE_MESH_ROWS = 2
NEG_FILL = -1e30

NN = (((1,), (0,)), ((), ()))
NT = (((1,), (1,)), ((), ()))
TN = (((0,), (0,)), ((), ()))


def mm(a, b, dims=NN):
    return lax.dot_general(a, b, dims, preferred_element_type=jnp.float32)


def attend_tiles(
    shape, slot_ref, q_ref, d_ref, k_ref, v_ref, att_ref, dq_ref, dk_ref, dv_ref, bias_ref
):
    mesh_rows, padded_cols, tile_points, head_size = shape
    tiles = mesh_rows // TILE_MESH_ROWS
    step_keys = TILE_MESH_ROWS * padded_cols
    keys = (TILE_MESH_ROWS + 2 * HALO_REACH) * padded_cols
    pair = 2 * head_size
    pairs = q_ref.shape[1] // pair
    scale = 1.0 / math.sqrt(head_size)
    low = (lax.broadcasted_iota(jnp.int32, (1, pair), 1) < head_size).astype(jnp.float32)
    high = (1.0 - low).astype(jnp.bfloat16)
    low = low.astype(jnp.bfloat16)
    dk_ref[...] = jnp.zeros_like(dk_ref)
    dv_ref[...] = jnp.zeros_like(dv_ref)

    def tile_step(tile, carry):
        rows = pl.ds(pl.multiple_of(tile * tile_points, tile_points), tile_points)
        window = pl.ds(pl.multiple_of(tile * step_keys, step_keys), keys)
        key_id = lax.broadcasted_iota(jnp.int32, (keys, tile_points), 0) + tile * step_keys
        linked = key_id == slot_ref[0:1, rows]
        for slot in range(1, EDGE_SLOTS):
            linked = linked | (key_id == slot_ref[slot : slot + 1, rows])
        bias_ref[...] = jnp.where(linked, 0.0, NEG_FILL)

        def split(block):
            return jnp.concatenate([block * low, block * high], axis=0)

        def joined(both):
            return jnp.concatenate(
                [both[:head_size, :tile_points], both[head_size:, tile_points:]], axis=0
            ).T

        def pair_step(index):
            lanes = pl.ds(pl.multiple_of(index * pair, pair), pair)
            q2 = split(q_ref[rows, lanes])
            d2 = split(d_ref[rows, lanes])
            k2 = k_ref[window, lanes]
            v2 = v_ref[window, lanes]
            bias = bias_ref[...]
            scores = mm(k2, q2, NT) + jnp.concatenate([bias, bias], axis=1)
            exps = jnp.exp(scores - jnp.max(scores, axis=0, keepdims=True))
            prob = exps * (1.0 / jnp.sum(exps, axis=0, keepdims=True))
            half = prob.astype(jnp.bfloat16)
            d_prob = mm(v2, d2, NT)
            centred = jnp.sum(prob * d_prob, axis=0, keepdims=True)
            d_score = (prob * (d_prob - centred)).astype(jnp.bfloat16)
            att_ref[rows, lanes] = joined(mm(v2, half, TN)).astype(att_ref.dtype)
            dq_ref[rows, lanes] = (joined(mm(k2, d_score, TN)) * scale).astype(dq_ref.dtype)
            dk_ref[window, lanes] += mm(d_score, q2)
            dv_ref[window, lanes] += mm(half, d2)

        def two_pairs(index, inner):
            pair_step(index * 2)
            pair_step(index * 2 + 1)
            return inner

        lax.fori_loop(0, pairs // 2, two_pairs, 0)
        return carry

    lax.fori_loop(0, tiles, tile_step, 0)


def attend_kernel(
    shape, slot_ref, q_ref, d_ref, k_ref, v_ref, att_ref, dq_ref, dk_out, dv_out, dk_ref, dv_ref, bias_ref
):
    attend_tiles(
        shape, slot_ref, q_ref, d_ref, k_ref, v_ref, att_ref, dq_ref, dk_ref, dv_ref, bias_ref
    )
    dk_out[...] = dk_ref[...].astype(dk_out.dtype)
    dv_out[...] = dv_ref[...].astype(dv_out.dtype)


def attend(shape, slots, queries, d_attended, keys, values):
    mesh_rows, padded_cols, tile_points, head_size = shape
    points, width = queries.shape
    window = (TILE_MESH_ROWS + 2 * HALO_REACH) * padded_cols
    vmem = pl.BlockSpec(memory_space=pltpu.VMEM)
    return pl.pallas_call(
        functools.partial(attend_kernel, shape),
        out_shape=(
            jax.ShapeDtypeStruct((points, width), jnp.bfloat16),
            jax.ShapeDtypeStruct((points, width), jnp.bfloat16),
            jax.ShapeDtypeStruct(keys.shape, jnp.bfloat16),
            jax.ShapeDtypeStruct(keys.shape, jnp.bfloat16),
        ),
        in_specs=[vmem] * 5,
        out_specs=(vmem,) * 4,
        scratch_shapes=[
            pltpu.VMEM(keys.shape, jnp.float32),
            pltpu.VMEM(keys.shape, jnp.float32),
            pltpu.VMEM((window, tile_points), jnp.float32),
        ],
        compiler_params=pltpu.CompilerParams(vmem_limit_bytes=40 * 2**20),
        cost_estimate=pl.CostEstimate(
            flops=12 * points * window * width,
            bytes_accessed=8 * points * width + 8 * keys.shape[0] * width,
            transcendentals=points * window * HEAD_COUNT,
        ),
    )(slots, queries, d_attended, keys, values)


def shifted(block, axis, step, periodic):
    count = lax.axis_size(axis)
    moves = []
    for source in range(count):
        target = source + step
        if periodic:
            moves.append((source, target % count))
        elif 0 <= target < count:
            moves.append((source, target))
    return lax.ppermute(block, axis, moves)


def local(grid_feat, mesh_feat, edges, edge_mask, w_query, w_key, w_value, w_out, cotangent):
    grid_rows, grid_cols, width = grid_feat.shape
    mesh_rows, mesh_cols, _ = mesh_feat.shape
    points = grid_rows * grid_cols
    head_size = width // HEAD_COUNT
    scale = 1.0 / math.sqrt(head_size)
    reach = HALO_REACH
    padded_rows = mesh_rows + 2 * reach
    padded_cols = mesh_cols + 2 * reach
    lon_total = mesh_cols * lax.axis_size("lon")
    tile_points = TILE_MESH_ROWS * (grid_rows // mesh_rows) * grid_cols
    shape = (mesh_rows, padded_cols, tile_points, head_size)

    below = shifted(mesh_feat[-reach:], "lat", 1, False)
    above = shifted(mesh_feat[:reach], "lat", -1, False)
    tall = jnp.concatenate([below, mesh_feat, above], axis=0)
    left = shifted(tall[:, -reach:], "lon", 1, True)
    right = shifted(tall[:, :reach], "lon", -1, True)
    padded_feat = jnp.concatenate([left, tall, right], axis=1).reshape(-1, width)

    lat_start = lax.axis_index("lat") * mesh_rows
    lon_start = lax.axis_index("lon") * mesh_cols
    targets = edges.reshape(EDGE_SLOTS, points)
    live = edge_mask.reshape(EDGE_SLOTS, points)
    target_lat = targets // lon_total - lat_start + reach
    target_lon = jnp.mod(targets % lon_total - lon_start + reach, lon_total)
    slots = jnp.where(live > 0, target_lat * padded_cols + target_lon, -1)

    grid_flat = grid_feat.reshape(points, width)
    cot_rows = cotangent.reshape(points, width)
    queries = (mm(grid_flat, w_query).astype(jnp.bfloat16).astype(jnp.float32) * scale).astype(
        jnp.bfloat16
    )
    d_attended = mm(cot_rows, w_out, NT).astype(jnp.bfloat16)
    keys = mm(padded_feat, w_key).astype(jnp.bfloat16)
    values = mm(padded_feat, w_value).astype(jnp.bfloat16)

    attended, d_query, d_keys, d_values = attend(shape, slots, queries, d_attended, keys, values)

    partial = (mm(d_keys, w_key, NT) + mm(d_values, w_value, NT)).reshape(
        padded_rows, padded_cols, width
    )
    rims = partial.astype(jnp.bfloat16)
    from_right = shifted(rims[:, :reach], "lon", -1, True).astype(jnp.float32)
    from_left = shifted(rims[:, -reach:], "lon", 1, True).astype(jnp.float32)
    middle = partial[:, reach:-reach]
    middle = middle + jnp.pad(from_left, ((0, 0), (0, mesh_cols - reach), (0, 0)))
    middle = middle + jnp.pad(from_right, ((0, 0), (mesh_cols - reach, 0), (0, 0)))
    lat_rims = middle.astype(jnp.bfloat16)
    from_above = shifted(lat_rims[:reach], "lat", -1, False).astype(jnp.float32)
    from_below = shifted(lat_rims[-reach:], "lat", 1, False).astype(jnp.float32)
    owned = middle[reach:-reach]
    owned = owned + jnp.pad(from_below, ((0, mesh_rows - reach), (0, 0), (0, 0)))
    owned = owned + jnp.pad(from_above, ((mesh_rows - reach, 0), (0, 0), (0, 0)))

    layer_out = (grid_flat.astype(jnp.float32) + mm(attended, w_out)).astype(jnp.bfloat16)
    grid_grad = (cot_rows.astype(jnp.float32) + mm(d_query, w_query, NT)).astype(jnp.bfloat16)
    return (
        layer_out.reshape(grid_feat.shape),
        grid_grad.reshape(grid_feat.shape),
        owned.astype(jnp.bfloat16),
    )


def solution(mesh):
    placed = (
        P("lat", "lon", None),
        P("lat", "lon", None),
        P(None, "lat", "lon"),
        P(None, "lat", "lon"),
        P(),
        P(),
        P(),
        P(),
        P("lat", "lon", None),
    )
    return jax.shard_map(
        local,
        mesh=mesh,
        in_specs=placed,
        out_specs=(P("lat", "lon", None), P("lat", "lon", None), P("lat", "lon", None)),
        check_vma=False,
    )
```

time: 156 us -> 69.1 us (0.44)
  the two profiles are of different devices: /device:TPU:4 before, /device:TPU:0 now
where the time goes in v1:
time: 69.1 us; the launch traced here: 68.6 us
  starting transfers between devices  20.4 us (30%)
  Pallas kernels  17.4 us (25%)
  matrix products  14 us (20%)
  waiting for transfers between devices  6.5 us (9%)
  local copies, waits for them, and re-layouts  6.47 us (9%)
  other arithmetic  2.97 us (4%)
  between operations  0.88 us (1%)
    ppermute x8, starting transfers between devices, shifted(): return lax.ppermute(block, axis, moves)  20.4 us
    pallas_call x1, Pallas kernels, attend(): pl.pallas_call(functools.partial(attend_kernel, shape), out_shape=(jax.Sh...  17.4 us
    dot_general x8, matrix products, mm(): return lax.dot_general(a, b, dims, preferred_element_type=jnp.float32)  14 us
    ppermute x8, waiting for transfers between devices, shifted(): return lax.ppermute(block, axis, moves)  6.5 us
    unnamed x22, local copies, waits for them, and re-layouts  1.96 us
    slice x1, local copies, waits for them, and re-layouts, local(): above = shifted(mesh_feat[:reach], 'lat', -1, False)  1.83 us
    reshape x1, local copies, waits for them, and re-layouts, local(): targets = edges.reshape(EDGE_SLOTS, points)  1.59 us
  transfers between devices with their start and end apart: 8, of which 3 were waited for; matrix products, arithmetic and copies ran while one was open for 22% of the time, Pallas kernels for 0%

profile of v1, /device:TPU:0, one launch (start us, length us, event | category | flops | bytes accessed | tf_op | source)
XLA Modules:
  0.0 68.6 jit_solution(17987905048454326015)
XLA Ops:
  0.6 0.0 copy-start
  0.6 1.8 %fusion.18 = (bf16[4,16,1024]{2,1,0:T(8,128)(2,1)}, bf16[4,16,1024]{2,1,0:T(8,128)(2,1)}) fusion(bf16[8,16,1024]{2,1,0:T(8,128)(2,1)} %param.10), kind=kLoop, calls=%fused_computation.41 | loop fusion | bytes 524288 | tf_op jit(solution)/shard_map/slice | solution.py:154
  2.5 1.3 %collective-permute-start.1 = (bf16[4,16,1024]{2,1,0:T(8,128)(2,1)}, bf16[4,16,1024]{2,1,0:T(8,128)(2,1)S(1)}, u32[]{:S(2)}, u32[]{:S(2)}) collective-permute-start(bf16[4,16,1024]{2,1,0:T(8,128)(2,1)} %get-tuple-element.19), channel_id=1, source_target_pairs={{8,0},{16,8},{24,16},{9,1},{17,9},{25,17},{10,2},{18,10},{26,18},{... | collective-permute-start | bytes 393224 | tf_op jit(solution)/shard_map/ppermute | solution.py:137
  3.8 6.1 %collective-permute-start = (bf16[4,16,1024]{2,1,0:T(8,128)(2,1)}, bf16[4,16,1024]{2,1,0:T(8,128)(2,1)}, u32[]{:S(2)}, u32[]{:S(2)}) collective-permute-start(bf16[4,16,1024]{2,1,0:T(8,128)(2,1)} %get-tuple-element.20), channel_id=1, source_target_pairs={{0,8},{8,16},{16,24},{1,9},{9,17},{17,25},{2,10},{10,18},{18,26},{... | collective-permute-start | bytes 393224 | tf_op jit(solution)/shard_map/ppermute | solution.py:137
  9.9 0.0 copy-start.8
  9.9 3.2 %multiply_convert_fusion.q_ref = bf16[512,1024]{1,0:T(8,128)(2,1)S(1)} fusion(bf16[512,1024]{1,0:T(8,128)(2,1)} %bitcast.26, bf16[1024,1024]{1,0:T(8,128)(2,1)} %param.13), kind=kOutput, calls=%fused_computation.2 | convolution fusion | flops 1075838976 | bytes 4194304 | tf_op jit(solution)/shard_map/dot_general | solution.py:23
  13.2 0.0 copy-done
  13.2 0.0 copy-done.8
  13.2 0.0 copy-start.4
  13.2 0.0 copy-start.3
  13.2 2.3 %convolution_convert_fusion.d_ref = bf16[512,1024]{1,0:T(8,128)(2,1)} fusion(bf16[512,1024]{1,0:T(8,128)(2,1)S(1)} %bitcast.28, bf16[1024,1024]{1,0:T(8,128)(2,1)S(1)} %copy-done), kind=kOutput, calls=%fused_computation.4 | convolution fusion | flops 1074266112 | bytes 4194304 | tf_op jit(solution)/shard_map/dot_general | solution.py:23
  15.5 0.0 copy-done.4
  15.5 0.6 broadcast_compare_fusion
  16.1 0.8 %gt.13 = pred[12,512]{1,0:T(8,128)(4,1)S(1)} reshape(pred[12,16,32]{2,1,0:T(8,128)(4,1)} %broadcast_compare_fusion) | data formatting | bytes 12288 | tf_op jit(solution)/shard_map/gt | solution.py:166
  16.9 1.6 %reshape.31 = s32[12,512]{1,0:T(8,128)} reshape(s32[12,16,32]{2,1,0:T(8,128)} %param.11) | data formatting | bytes 49152 | tf_op jit(solution)/shard_map/reshape | solution.py:162
  18.5 0.0 copy-start.2
  18.5 0.0 collective-permute-done
  18.5 1.1 %constant_dynamic-update-slice_fusion.2 = bf16[16,16,1024]{2,1,0:T(8,128)(2,1)S(1)} fusion(bf16[4,16,1024]{2,1,0:T(8,128)(2,1)} %collective-permute-done), kind=kLoop, calls=%fused_computation.36 | loop fusion | bytes 262144
  19.6 0.0 copy-done.3
  19.6 0.0 collective-permute-done.1
  19.6 0.1 fusion.17
  19.8 0.1 collective-permute-start.2
  19.8 3.5 %collective-permute-start.3 = (bf16[16,4,1024]{2,1,0:T(4,128)(2,1)S(1)}, bf16[16,4,1024]{2,1,0:T(4,128)(2,1)S(1)}, u32[]{:S(2)}, u32[]{:S(2)}) collective-permute-start(bf16[16,4,1024]{2,1,0:T(4,128)(2,1)S(1)} %get-tuple-element.18), channel_id=1, source_target_pairs={{0,7},{1,0},{2,1},{3,2},{4,3},{5,4},{6,5},{7,6},{8,15},{9,8},{10,9... | collective-permute-start | bytes 393224 | tf_op jit(solution)/shard_map/ppermute | solution.py:137
  23.4 0.8 %fusion.7.slot_ref = s32[12,512]{1,0:T(8,128)S(1)} fusion(pred[12,512]{1,0:T(8,128)(4,1)S(1)} %gt.13, s32[12,512]{1,0:T(8,128)} %reshape.31, s32[]{:T(128)S(6)} %mul.21, s32[]{:T(128)S(6)} %mul.18), kind=kLoop, calls=%fused_computation.27 | loop fusion | flops 227328 | bytes 55304 | tf_op jit(solution)/shard_map/jit(_where)/select_n | solution.py:166
  24.2 1.9 %collective-permute-done.2 = bf16[16,4,1024]{2,1,0:T(4,128)(2,1)S(1)} collective-permute-done((bf16[16,4,1024]{2,1,0:T(4,128)(2,1)S(1)}, bf16[16,4,1024]{2,1,0:T(4,128)(2,1)S(1)}, u32[]{:S(2)}, u32[]{:S(2)}) %collective-permute-start.2) | collective-permute-done | bytes 131104 | tf_op jit(solution)/shard_map/ppermute | solution.py:137
  26.1 0.0 collective-permute-done.3
  26.1 0.4 pad_maximum_fusion
  26.5 0.0 copy-done.2
  26.5 0.0 copy-start.5
  26.5 1.0 %convolution_convert_fusion.2.v_ref = bf16[384,1024]{1,0:T(8,128)(2,1)S(1)} fusion(bf16[384,1024]{1,0:T(8,128)(2,1)S(1)} %bitcast.24, bf16[1024,1024]{1,0:T(8,128)(2,1)S(1)} %copy-done.2), kind=kOutput, calls=%fused_computation.6 | convolution fusion | flops 805699584 | bytes 3670016 | tf_op jit(solution)/shard_map/dot_general | solution.py:23
  27.5 0.6 copy-done.5
  28.1 0.0 copy-start.1
  28.1 1.0 %convolution_convert_fusion.3.k_ref = bf16[384,1024]{1,0:T(8,128)(2,1)S(1)} fusion(bf16[384,1024]{1,0:T(8,128)(2,1)S(1)} %bitcast.25, bf16[1024,1024]{1,0:T(8,128)(2,1)S(1)} %copy-done.5), kind=kOutput, calls=%fused_computation.7 | convolution fusion | flops 805699584 | bytes 3670016 | tf_op jit(solution)/shard_map/dot_general | solution.py:23
  29.1 0.2 copy-done.1
  29.3 17.4 %shard_map.112 = (bf16[512,1024]{1,0:T(8,128)(2,1)S(1)}, bf16[512,1024]{1,0:T(8,128)(2,1)S(1)}, bf16[384,1024]{1,0:T(8,128)(2,1)S(1)}, bf16[384,1024]{1,0:T(8,128)(2,1)S(1)}) custom-call(s32[12,512]{1,0:T(8,128)S(1)} %fusion.7.slot_ref, bf16[512,1024]{1,0:T(8,128)(2,1)S(1)} %multiply_convert_fusion.q_ref, bf16[512,1024]{1,0:T(8,128)(2,1)S(1)} %copy-done.1, ...), custom_call_target="tpu_custom_call" | custom-call | flops 1509949440 | bytes 7340032 | tf_op jit(solution)/shard_map/pallas_call | solution.py:104
  46.7 1.0 %fusion.19 = f32[384,1024]{1,0:T(8,128)S(1)} fusion(bf16[384,1024]{1,0:T(8,128)(2,1)S(1)} %get-tuple-element.9, bf16[1024,1024]{1,0:T(8,128)(2,1)S(1)} %copy-done.5), kind=kOutput, calls=%fused_computation.42 | convolution fusion | flops 805306368 | bytes 4456448 | tf_op jit(solution)/shard_map/dot_general | solution.py:23
  47.7 1.0 %convolution_add_fusion = f32[384,1024]{1,0:T(8,128)S(1)} fusion(f32[384,1024]{1,0:T(8,128)S(1)} %fusion.19, bf16[384,1024]{1,0:T(8,128)(2,1)S(1)} %get-tuple-element.10, bf16[1024,1024]{1,0:T(8,128)(2,1)S(1)} %copy-done.2), kind=kOutput, calls=%fused_computation.3 | convolution fusion | flops 805699584 | bytes 6029312 | tf_op jit(solution)/shard_map/dot_general | solution.py:23
  48.8 0.0 copy-start.7
  48.8 0.1 convert_element_type.61
  48.9 0.1 fusion.15
  49.0 1.2 %collective-permute-start.4 = (bf16[16,4,1024]{2,1,0:T(4,128)(2,1)S(1)}, bf16[16,4,1024]{2,1,0:T(4,128)(2,1)S(1)}, u32[]{:S(2)}, u32[]{:S(2)}) collective-permute-start(bf16[16,4,1024]{2,1,0:T(4,128)(2,1)S(1)} %get-tuple-element.13), channel_id=1, source_target_pairs={{0,1},{1,2},{2,3},{3,4},{4,5},{5,6},{6,7},{7,0},{8,9},{9,10},{10,1... | collective-permute-start | bytes 393224 | tf_op jit(solution)/shard_map/ppermute | solution.py:137
  50.2 2.4 %collective-permute-start.5 = (bf16[16,4,1024]{2,1,0:T(4,128)(2,1)S(1)}, bf16[16,4,1024]{2,1,0:T(4,128)(2,1)S(1)}, u32[]{:S(2)}, u32[]{:S(2)}) collective-permute-start(bf16[16,4,1024]{2,1,0:T(4,128)(2,1)S(1)} %get-tuple-element.14), channel_id=1, source_target_pairs={{0,7},{1,0},{2,1},{3,2},{4,3},{5,4},{6,5},{7,6},{8,15},{9,8},{10,9... | collective-permute-start | bytes 393224 | tf_op jit(solution)/shard_map/ppermute | solution.py:137
  52.6 0.0 copy-done.7
  52.6 2.2 %add_convert_fusion.1 = bf16[512,1024]{1,0:T(8,128)(2,1)} fusion(bf16[512,1024]{1,0:T(8,128)(2,1)S(1)} %bitcast.27, bf16[512,1024]{1,0:T(8,128)(2,1)S(1)} %get-tuple-element.7, bf16[1024,1024]{1,0:T(8,128)(2,1)S(1)} %copy-done), kind=kOutput, calls=%fused_computation.1 | convolution fusion | flops 1075314688 | bytes 5242880 | tf_op jit(solution)/shard_map/dot_general | solution.py:23
  54.8 0.0 copy-start.6
  54.8 0.0 copy-start.9
  54.8 1.0 %collective-permute-done.4 = bf16[16,4,1024]{2,1,0:T(4,128)(2,1)S(1)} collective-permute-done((bf16[16,4,1024]{2,1,0:T(4,128)(2,1)S(1)}, bf16[16,4,1024]{2,1,0:T(4,128)(2,1)S(1)}, u32[]{:S(2)}, u32[]{:S(2)}) %collective-permute-start.4) | collective-permute-done | bytes 131104 | tf_op jit(solution)/shard_map/ppermute | solution.py:137
  55.9 0.0 collective-permute-done.5
  55.9 0.3 fusion.13
  56.2 4.5 %collective-permute-start.6 = (bf16[4,16,1024]{2,1,0:T(8,128)(2,1)S(1)}, bf16[4,16,1024]{2,1,0:T(8,128)(2,1)S(1)}, u32[]{:S(2)}, u32[]{:S(2)}) collective-permute-start(bf16[4,16,1024]{2,1,0:T(8,128)(2,1)S(1)} %get-tuple-element.15), channel_id=1, source_target_pairs={{0,8},{8,16},{16,24},{1,9},{9,17},{17,25},{2,10},{10,18},{18,26},{... | collective-permute-start | bytes 393224 | tf_op jit(solution)/shard_map/ppermute | solution.py:137
  60.7 1.3 %collective-permute-start.7 = (bf16[4,16,1024]{2,1,0:T(8,128)(2,1)S(1)}, bf16[4,16,1024]{2,1,0:T(8,128)(2,1)S(1)}, u32[]{:S(2)}, u32[]{:S(2)}) collective-permute-start(bf16[4,16,1024]{2,1,0:T(8,128)(2,1)S(1)} %get-tuple-element.16), channel_id=1, source_target_pairs={{8,0},{16,8},{24,16},{9,1},{17,9},{25,17},{10,2},{18,10},{26,18},{... | collective-permute-start | bytes 393224 | tf_op jit(solution)/shard_map/ppermute | solution.py:137
  62.0 0.0 copy-done.6
  62.0 0.0 copy-done.9
  62.0 2.3 %add_convert_fusion = bf16[512,1024]{1,0:T(8,128)(2,1)} fusion(bf16[512,1024]{1,0:T(8,128)(2,1)S(1)} %bitcast.29, bf16[512,1024]{1,0:T(8,128)(2,1)S(1)} %get-tuple-element.8, bf16[1024,1024]{1,0:T(8,128)(2,1)S(1)} %copy-done.6), kind=kOutput, calls=%fused_computation | convolution fusion | flops 1075314688 | bytes 5242880 | tf_op jit(solution)/shard_map/dot_general | solution.py:23
  64.3 0.0 collective-permute-done.6
  64.3 3.5 %collective-permute-done.7 = bf16[4,16,1024]{2,1,0:T(8,128)(2,1)S(1)} collective-permute-done((bf16[4,16,1024]{2,1,0:T(8,128)(2,1)S(1)}, bf16[4,16,1024]{2,1,0:T(8,128)(2,1)S(1)}, u32[]{:S(2)}, u32[]{:S(2)}) %collective-permute-start.7) | collective-permute-done | bytes 131104 | tf_op jit(solution)/shard_map/ppermute | solution.py:137
  67.8 0.8 %fusion.2 = bf16[8,16,1024]{2,1,0:T(8,128)(2,1)} fusion(f32[16,16,1024]{2,1,0:T(8,128)S(1)} %get-tuple-element.12, bf16[4,16,1024]{2,1,0:T(8,128)(2,1)S(1)} %collective-permute-done.7, bf16[4,16,1024]{2,1,0:T(8,128)(2,1)S(1)} %collective-permute-done.6), kind=kLoop, calls=%fused_computation.13 | loop fusion | flops 655360 | bytes 1048576 | tf_op jit(solution)/shard_map/convert_element_type | solution.py:200
  (3 shorter events, 0.1 us)
Async XLA Ops:
  0.6 12.5 %copy-start = (bf16[1024,1024]{1,0:T(8,128)(2,1)S(1)}, bf16[1024,1024]{1,0:T(8,128)(2,1)}, u32[]{:S(2)}) copy-start(bf16[1024,1024]{1,0:T(8,128)(2,1)} %param.16) | copy-start | bytes 6291460
  2.5 17.1 %collective-permute-start.1 = (bf16[4,16,1024]{2,1,0:T(8,128)(2,1)}, bf16[4,16,1024]{2,1,0:T(8,128)(2,1)S(1)}, u32[]{:S(2)}, u32[]{:S(2)}) collective-permute-start(bf16[4,16,1024]{2,1,0:T(8,128)(2,1)} %get-tuple-element.19), channel_id=1, source_target_pairs={{8,0},{16,8},{24,16},{9,1},{17,9},{25,17},{10,2},{18,10},{26,18},{... | collective-permute-start | bytes 393224 | tf_op jit(solution)/shard_map/ppermute | solution.py:137
  3.8 14.7 %collective-permute-start = (bf16[4,16,1024]{2,1,0:T(8,128)(2,1)}, bf16[4,16,1024]{2,1,0:T(8,128)(2,1)}, u32[]{:S(2)}, u32[]{:S(2)}) collective-permute-start(bf16[4,16,1024]{2,1,0:T(8,128)(2,1)} %get-tuple-element.20), channel_id=1, source_target_pairs={{0,8},{8,16},{16,24},{1,9},{9,17},{17,25},{2,10},{10,18},{18,26},{... | collective-permute-start | bytes 393224 | tf_op jit(solution)/shard_map/ppermute | solution.py:137
  9.9 3.3 %copy-start.8 = (bf16[16,32,1024]{2,1,0:T(8,128)(2,1)S(1)}, bf16[16,32,1024]{2,1,0:T(8,128)(2,1)}, u32[]{:S(2)}) copy-start(bf16[16,32,1024]{2,1,0:T(8,128)(2,1)} %param.17) | copy-start | bytes 3145732
  13.2 2.3 %copy-start.4 = (s32[12,16,32]{2,1,0:T(8,128)S(1)}, s32[12,16,32]{2,1,0:T(8,128)}, u32[]{:S(2)}) copy-start(s32[12,16,32]{2,1,0:T(8,128)} %param.12) | copy-start | bytes 73732
  13.2 6.4 %copy-start.3 = (bf16[8,16,1024]{2,1,0:T(8,128)(2,1)S(1)}, bf16[8,16,1024]{2,1,0:T(8,128)(2,1)}, u32[]{:S(2)}) copy-start(bf16[8,16,1024]{2,1,0:T(8,128)(2,1)} %param.10) | copy-start | bytes 786436
  18.5 8.0 %copy-start.2 = (bf16[1024,1024]{1,0:T(8,128)(2,1)S(1)}, bf16[1024,1024]{1,0:T(8,128)(2,1)}, u32[]{:S(2)}) copy-start(bf16[1024,1024]{1,0:T(8,128)(2,1)} %param.15) | copy-start | bytes 6291460
  19.8 6.3 %collective-permute-start.2 = (bf16[16,4,1024]{2,1,0:T(4,128)(2,1)S(1)}, bf16[16,4,1024]{2,1,0:T(4,128)(2,1)S(1)}, u32[]{:S(2)}, u32[]{:S(2)}) collective-permute-start(bf16[16,4,1024]{2,1,0:T(4,128)(2,1)S(1)} %get-tuple-element.17), channel_id=1, source_target_pairs={{0,1},{1,2},{2,3},{3,4},{4,5},{5,6},{6,7},{7,0},{8,9},{9,10},{10,1... | collective-permute-start | bytes 393224 | tf_op jit(solution)/shard_map/ppermute | solution.py:137
  19.8 6.3 %collective-permute-start.3 = (bf16[16,4,1024]{2,1,0:T(4,128)(2,1)S(1)}, bf16[16,4,1024]{2,1,0:T(4,128)(2,1)S(1)}, u32[]{:S(2)}, u32[]{:S(2)}) collective-permute-start(bf16[16,4,1024]{2,1,0:T(4,128)(2,1)S(1)} %get-tuple-element.18), channel_id=1, source_target_pairs={{0,7},{1,0},{2,1},{3,2},{4,3},{5,4},{6,5},{7,6},{8,15},{9,8},{10,9... | collective-permute-start | bytes 393224 | tf_op jit(solution)/shard_map/ppermute | solution.py:137
  26.5 1.6 %copy-start.5 = (bf16[1024,1024]{1,0:T(8,128)(2,1)S(1)}, bf16[1024,1024]{1,0:T(8,128)(2,1)}, u32[]{:S(2)}) copy-start(bf16[1024,1024]{1,0:T(8,128)(2,1)} %param.14) | copy-start | bytes 6291460
  28.1 1.2 %copy-start.1 = (bf16[512,1024]{1,0:T(8,128)(2,1)S(1)}, bf16[512,1024]{1,0:T(8,128)(2,1)}, u32[]{:S(2)}) copy-start(bf16[512,1024]{1,0:T(8,128)(2,1)} %convolution_convert_fusion.d_ref) | copy-start | bytes 3145732
  48.8 3.8 %copy-start.7 = (bf16[16,32,1024]{2,1,0:T(8,128)(2,1)S(1)}, bf16[16,32,1024]{2,1,0:T(8,128)(2,1)}, u32[]{:S(2)}) copy-start(bf16[16,32,1024]{2,1,0:T(8,128)(2,1)} %param.9) | copy-start | bytes 3145732
  49.0 6.9 %collective-permute-start.4 = (bf16[16,4,1024]{2,1,0:T(4,128)(2,1)S(1)}, bf16[16,4,1024]{2,1,0:T(4,128)(2,1)S(1)}, u32[]{:S(2)}, u32[]{:S(2)}) collective-permute-start(bf16[16,4,1024]{2,1,0:T(4,128)(2,1)S(1)} %get-tuple-element.13), channel_id=1, source_target_pairs={{0,1},{1,2},{2,3},{3,4},{4,5},{5,6},{6,7},{7,0},{8,9},{9,10},{10,1... | collective-permute-start | bytes 393224 | tf_op jit(solution)/shard_map/ppermute | solution.py:137
  50.2 5.7 %collective-permute-start.5 = (bf16[16,4,1024]{2,1,0:T(4,128)(2,1)S(1)}, bf16[16,4,1024]{2,1,0:T(4,128)(2,1)S(1)}, u32[]{:S(2)}, u32[]{:S(2)}) collective-permute-start(bf16[16,4,1024]{2,1,0:T(4,128)(2,1)S(1)} %get-tuple-element.14), channel_id=1, source_target_pairs={{0,7},{1,0},{2,1},{3,2},{4,3},{5,4},{6,5},{7,6},{8,15},{9,8},{10,9... | collective-permute-start | bytes 393224 | tf_op jit(solution)/shard_map/ppermute | solution.py:137
  54.8 7.2 %copy-start.6 = (bf16[1024,1024]{1,0:T(8,128)(2,1)S(1)}, bf16[1024,1024]{1,0:T(8,128)(2,1)}, u32[]{:S(2)}) copy-start(bf16[1024,1024]{1,0:T(8,128)(2,1)} %param.13) | copy-start | bytes 6291460
  54.8 7.2 %copy-start.9 = (bf16[16,32,1024]{2,1,0:T(8,128)(2,1)S(1)}, bf16[16,32,1024]{2,1,0:T(8,128)(2,1)}, u32[]{:S(2)}) copy-start(bf16[16,32,1024]{2,1,0:T(8,128)(2,1)} %param.17) | copy-start | bytes 3145732
  56.2 8.1 %collective-permute-start.6 = (bf16[4,16,1024]{2,1,0:T(8,128)(2,1)S(1)}, bf16[4,16,1024]{2,1,0:T(8,128)(2,1)S(1)}, u32[]{:S(2)}, u32[]{:S(2)}) collective-permute-start(bf16[4,16,1024]{2,1,0:T(8,128)(2,1)S(1)} %get-tuple-element.15), channel_id=1, source_target_pairs={{0,8},{8,16},{16,24},{1,9},{9,17},{17,25},{2,10},{10,18},{18,26},{... | collective-permute-start | bytes 393224 | tf_op jit(solution)/shard_map/ppermute | solution.py:137
  60.7 7.1 %collective-permute-start.7 = (bf16[4,16,1024]{2,1,0:T(8,128)(2,1)S(1)}, bf16[4,16,1024]{2,1,0:T(8,128)(2,1)S(1)}, u32[]{:S(2)}, u32[]{:S(2)}) collective-permute-start(bf16[4,16,1024]{2,1,0:T(8,128)(2,1)S(1)} %get-tuple-element.16), channel_id=1, source_target_pairs={{8,0},{16,8},{24,16},{9,1},{17,9},{25,17},{10,2},{18,10},{26,18},{... | collective-permute-start | bytes 393224 | tf_op jit(solution)/shard_map/ppermute | solution.py:137

commit v2 on v1

v2 whole, which is shorter than its diff:
```python
import functools
import math

import jax
import jax.numpy as jnp
from jax import lax
from jax.experimental import pallas as pl
from jax.experimental.pallas import tpu as pltpu
from jax.sharding import PartitionSpec as P

HEAD_COUNT = 16
EDGE_SLOTS = 12
HALO_REACH = 4
TILE_MESH_ROWS = 2
ROW_GROUP = 16
PAIRS_UNROLLED = 4
NEG_FILL = -1e30

NN = (((1,), (0,)), ((), ()))
NT = (((1,), (1,)), ((), ()))
TN = (((0,), (0,)), ((), ()))


def mm(a, b, dims=NN):
    return lax.dot_general(a, b, dims, preferred_element_type=jnp.float32)


class Plan:
    def __init__(self, mesh_rows, mesh_cols, grid_rows, grid_cols, width, lat_count, lon_count):
        reach = HALO_REACH
        self.mesh_rows, self.mesh_cols = mesh_rows, mesh_cols
        self.grid_rows, self.grid_cols, self.width = grid_rows, grid_cols, width
        self.lat_count, self.lon_count = lat_count, lon_count
        self.head = width // HEAD_COUNT
        self.scale = 1.0 / math.sqrt(self.head)
        self.points = grid_rows * grid_cols
        self.own = mesh_rows * mesh_cols
        padded_rows = mesh_rows + 2 * reach
        self.mid = padded_rows * mesh_cols
        self.strip = padded_rows * reach
        self.nodes = self.mid + 2 * self.strip
        self.lat_rim = reach * mesh_cols
        self.lon_rim = mesh_rows * reach
        self.corner = reach * reach
        self.tiles = mesh_rows // TILE_MESH_ROWS
        self.tile_grid_rows = grid_rows // self.tiles
        self.tile_points = self.tile_grid_rows * grid_cols
        window_rows = TILE_MESH_ROWS + 2 * reach
        self.mid_step = TILE_MESH_ROWS * mesh_cols
        self.mid_keys = window_rows * mesh_cols
        self.side_step = TILE_MESH_ROWS * reach
        slack = max((tile * self.side_step) % ROW_GROUP for tile in range(self.tiles))
        covered = window_rows * reach + slack
        self.side_keys = min(self.strip, -(-covered // ROW_GROUP) * ROW_GROUP)
        self.keys = self.mid_keys + 2 * self.side_keys

    def side_start(self, tile):
        return (tile * self.side_step) // ROW_GROUP * ROW_GROUP

    def exchanges(self):
        mid, strip = self.mid, self.strip
        corner, lon_rim, lat_rim = self.corner, self.lon_rim, self.lat_rim
        left, right = mid, mid + strip
        return (
            (-1, 0, 0, lat_rim),
            (1, 0, mid - lat_rim, lat_rim),
            (0, -1, left + corner, lon_rim),
            (0, 1, right + corner, lon_rim),
            (-1, -1, left, corner),
            (1, -1, left + strip - corner, corner),
            (-1, 1, right, corner),
            (1, 1, right + strip - corner, corner),
        )


def pack_matrix(plan):
    rows = 2 * plan.lon_rim
    row = lax.broadcasted_iota(jnp.int32, (rows, plan.own), 0)
    node = lax.broadcasted_iota(jnp.int32, (rows, plan.own), 1)
    is_right = (row >= plan.lon_rim).astype(jnp.int32)
    within = row - is_right * plan.lon_rim
    mesh_row = within // HALO_REACH
    col = within - mesh_row * HALO_REACH + is_right * (plan.mesh_cols - HALO_REACH)
    hit = node == mesh_row * plan.mesh_cols + col
    return hit.astype(jnp.float32).astype(jnp.bfloat16)


def fill_slots(plan, lat_start, lon_start, edges_ref, mask_ref, slot_ref):
    reach, cols = HALO_REACH, plan.mesh_cols
    lon_total = plan.mesh_cols * plan.lon_count
    for tile in range(plan.tiles):
        rows = range(tile * plan.tile_grid_rows, (tile + 1) * plan.tile_grid_rows)
        target = jnp.concatenate([edges_ref[:, row, :] for row in rows], axis=1)
        live = jnp.concatenate([mask_ref[:, row, :] for row in rows], axis=1)
        if lon_total & (lon_total - 1):
            node_row = lax.div(target, jnp.full_like(target, lon_total))
        else:
            node_row = lax.shift_right_logical(
                target, jnp.full_like(target, lon_total.bit_length() - 1)
            )
        node_col = target - node_row * lon_total - lon_start + reach
        node_col = jnp.where(node_col < 0, node_col + lon_total, node_col)
        node_col = jnp.where(node_col >= lon_total, node_col - lon_total, node_col)
        node_row = node_row - lat_start + reach
        side = plan.mid_keys + node_row * reach - plan.side_start(tile)
        middle = node_row * cols + node_col - reach - tile * plan.mid_step
        right = side + plan.side_keys + node_col - cols - reach
        slot = jnp.where(
            node_col < reach, side + node_col, jnp.where(node_col < cols + reach, middle, right)
        )
        slot_ref[tile] = jnp.where(live > 0, slot, -1)


def attend_tiles(
    plan, slot_ref, q_ref, d_ref, k_ref, v_ref, att_ref, dq_ref, dk_ref, dv_ref, bias_ref
):
    head, tile_points = plan.head, plan.tile_points
    pair = 2 * head
    pairs = plan.width // pair
    low = (lax.broadcasted_iota(jnp.int32, (1, pair), 1) < head).astype(jnp.float32)
    high = (1.0 - low).astype(jnp.bfloat16)
    low = low.astype(jnp.bfloat16)
    dk_ref[...] = jnp.zeros_like(dk_ref)
    dv_ref[...] = jnp.zeros_like(dv_ref)

    def tile_step(tile, carry):
        rows = pl.ds(pl.multiple_of(tile * tile_points, tile_points), tile_points)
        side = plan.side_start(tile)
        windows = (
            (pl.ds(pl.multiple_of(tile * plan.mid_step, ROW_GROUP), plan.mid_keys), 0),
            (pl.ds(pl.multiple_of(plan.mid + side, ROW_GROUP), plan.side_keys), plan.mid_keys),
            (
                pl.ds(pl.multiple_of(plan.mid + plan.strip + side, ROW_GROUP), plan.side_keys),
                plan.mid_keys + plan.side_keys,
            ),
        )
        key_id = lax.broadcasted_iota(jnp.int32, (plan.keys, tile_points), 0)
        slots = slot_ref[tile]
        linked = key_id == slots[0:1]
        for slot in range(1, EDGE_SLOTS):
            linked = linked | (key_id == slots[slot : slot + 1])
        bias_ref[...] = jnp.where(linked, 0.0, NEG_FILL)

        def split(block):
            return jnp.concatenate([block * low, block * high], axis=0)

        def joined(both):
            return jnp.concatenate([both[:head, :tile_points], both[head:, tile_points:]], axis=0).T

        def window_of(ref, lanes):
            return jnp.concatenate([ref[window, lanes] for window, _ in windows], axis=0)

        def add_window(ref, lanes, block):
            for window, first in windows:
                ref[window, lanes] += block[first : first + window.size]

        def pair_step(index):
            lanes = pl.ds(pl.multiple_of(index * pair, pair), pair)
            q2 = split(q_ref[rows, lanes])
            d2 = split(d_ref[rows, lanes])
            k2 = window_of(k_ref, lanes)
            v2 = window_of(v_ref, lanes)
            bias = bias_ref[...]
            scores = mm(k2, q2, NT) + jnp.concatenate([bias, bias], axis=1)
            exps = jnp.exp(scores - jnp.max(scores, axis=0, keepdims=True))
            prob = exps * (1.0 / jnp.sum(exps, axis=0, keepdims=True))
            half = prob.astype(jnp.bfloat16)
            d_prob = mm(v2, d2, NT)
            centred = jnp.sum(prob * d_prob, axis=0, keepdims=True)
            d_score = (prob * (d_prob - centred)).astype(jnp.bfloat16)
            att_ref[rows, lanes] = joined(mm(v2, half, TN)).astype(att_ref.dtype)
            dq_ref[rows, lanes] = (joined(mm(k2, d_score, TN)) * plan.scale).astype(dq_ref.dtype)
            add_window(dk_ref, lanes, mm(d_score, q2))
            add_window(dv_ref, lanes, mm(half, d2))

        def some_pairs(index, inner):
            for offset in range(PAIRS_UNROLLED):
                pair_step(index * PAIRS_UNROLLED + offset)
            return inner

        lax.fori_loop(0, pairs // PAIRS_UNROLLED, some_pairs, 0)
        return carry

    lax.fori_loop(0, plan.tiles, tile_step, 0)


def column_tiles(width, body):
    tile = min(width, 256)

    def step(index, carry):
        body(pl.ds(pl.multiple_of(index * tile, tile), tile))
        return carry

    lax.fori_loop(0, width // tile, step, 0)


def layer_kernel(
    plan,
    grid_in, mesh_in, edges_in, mask_in, wq_in, wk_in, wv_in, wo_in, cot_in,
    out_ref, grid_grad_ref, mesh_grad_ref,
    grid_ref, cot_ref, edges_ref, mask_ref, wq_ref, wk_ref, wv_ref, wo_ref,
    feat_ref, pack_ref, slot_ref, q_ref, d_ref, k_ref, v_ref, att_ref, dq_ref,
    dk_ref, dv_ref, bias_ref, own_ref, part_ref, back_ref,
    load_sem, send_sem, recv_sem, back_send_sem, back_recv_sem,
):
    reach = HALO_REACH
    lat, lon = lax.axis_index("lat"), lax.axis_index("lon")
    exchanges = plan.exchanges()
    first_own = plan.lat_rim

    def device(lat_step, lon_step):
        return (
            lax.rem(lat + lat_step + plan.lat_count, plan.lat_count),
            lax.rem(lon + lon_step + plan.lon_count, plan.lon_count),
        )

    barrier = pltpu.get_barrier_semaphore()
    for lat_step, lon_step, _, _ in exchanges:
        pl.semaphore_signal(
            barrier, inc=1, device_id=device(lat_step, lon_step), device_id_type=pl.DeviceIdType.MESH
        )
    own_feat = feat_ref.at[pl.ds(first_own, plan.own)]
    loads = []
    for index, (source, target) in enumerate(
        (
            (mesh_in, own_feat), (grid_in, grid_ref), (wq_in, wq_ref), (edges_in, edges_ref),
            (mask_in, mask_ref), (cot_in, cot_ref), (wo_in, wo_ref), (wk_in, wk_ref),
            (wv_in, wv_ref),
        )
    ):
        load = pltpu.make_async_copy(source, target, load_sem.at[index])
        load.start()
        loads.append(load)
    mesh_load, grid_load, wq_load, edges_load, mask_load, cot_load, wo_load, wk_load, wv_load = loads

    mesh_load.wait()
    pack = pack_matrix(plan)
    pack_ref[...] = mm(pack, own_feat[...]).astype(jnp.bfloat16)
    pl.semaphore_wait(barrier, len(exchanges))
    corner, lon_rim = plan.corner, plan.lon_rim
    sent = []
    for index, (lat_step, lon_step, first, count) in enumerate(exchanges):
        if lon_step == 0:
            start = first_own + (plan.own - count if lat_step < 0 else 0)
            source = feat_ref.at[pl.ds(start, count)]
        else:
            start = lon_rim if lon_step < 0 else 0
            if lat_step < 0:
                start += lon_rim - count
            source = pack_ref.at[pl.ds(start, count)]
        copy = pltpu.make_async_remote_copy(
            src_ref=source,
            dst_ref=feat_ref.at[pl.ds(first, count)],
            send_sem=send_sem.at[index],
            recv_sem=recv_sem.at[index],
            device_id=device(-lat_step, -lon_step),
            device_id_type=pl.DeviceIdType.MESH,
        )
        copy.start()
        sent.append(copy)

    grid_load.wait()
    wq_load.wait()

    def query_columns(columns):
        queries = mm(grid_ref[...], wq_ref[:, columns]).astype(jnp.bfloat16)
        q_ref[:, columns] = (queries.astype(jnp.float32) * plan.scale).astype(jnp.bfloat16)

    column_tiles(plan.width, query_columns)
    edges_load.wait()
    mask_load.wait()
    fill_slots(
        plan, lat * plan.mesh_rows, lon * plan.mesh_cols, edges_ref, mask_ref, slot_ref
    )
    cot_load.wait()
    wo_load.wait()

    def d_columns(columns):
        d_ref[:, columns] = mm(cot_ref[...], wo_ref[columns, :], NT).astype(jnp.bfloat16)

    column_tiles(plan.width, d_columns)
    wk_load.wait()
    wv_load.wait()
    for copy in sent:
        copy.wait()

    def pair_columns(columns):
        feat = feat_ref[...]
        k_ref[:, columns] = mm(feat, wk_ref[:, columns]).astype(jnp.bfloat16)
        v_ref[:, columns] = mm(feat, wv_ref[:, columns]).astype(jnp.bfloat16)

    column_tiles(plan.width, pair_columns)
    attend_tiles(
        plan, slot_ref, q_ref, d_ref, k_ref, v_ref, att_ref, dq_ref, dk_ref, dv_ref, bias_ref
    )
    k_ref[...] = dk_ref[...].astype(jnp.bfloat16)
    v_ref[...] = dv_ref[...].astype(jnp.bfloat16)

    def part_columns(columns):
        part = mm(k_ref[...], wk_ref[columns, :], NT) + mm(v_ref[...], wv_ref[columns, :], NT)
        part_ref[:, columns] = part.astype(jnp.bfloat16)
        own_ref[:, columns] = part[first_own : first_own + plan.own]

    column_tiles(plan.width, part_columns)
    returned = []
    for index, (lat_step, lon_step, first, count) in enumerate(exchanges):
        if lon_step == 0:
            start = count if lat_step < 0 else 0
        else:
            base = 2 * plan.lat_rim
            if lat_step == 0:
                start = base + (lon_rim if lon_step < 0 else 0)
            else:
                base += 2 * lon_rim
                order = (0 if lon_step > 0 else 2) + (1 if lat_step < 0 else 0)
                start = base + order * corner
        copy = pltpu.make_async_remote_copy(
            src_ref=part_ref.at[pl.ds(first, count)],
            dst_ref=back_ref.at[pl.ds(start, count)],
            send_sem=back_send_sem.at[index],
            recv_sem=back_recv_sem.at[index],
            device_id=device(lat_step, lon_step),
            device_id_type=pl.DeviceIdType.MESH,
        )
        copy.start()
        returned.append(copy)

    def out_columns(columns):
        out = grid_ref[:, columns].astype(jnp.float32) + mm(att_ref[...], wo_ref[:, columns])
        out_ref[:, columns] = out.astype(jnp.bfloat16)
        grad = cot_ref[:, columns].astype(jnp.float32) + mm(dq_ref[...], wq_ref[columns, :], NT)
        grid_grad_ref[:, columns] = grad.astype(jnp.bfloat16)

    column_tiles(plan.width, out_columns)
    for copy in returned:
        copy.wait()
    corners = [
        pack[0:corner], pack[lon_rim - corner : lon_rim],
        pack[lon_rim : lon_rim + corner], pack[2 * lon_rim - corner : 2 * lon_rim],
    ]
    unpack = jnp.concatenate([pack] + corners, axis=0)
    lat_terms = 2 * plan.lat_rim
    last_rim = pl.ds(plan.own - plan.lat_rim, plan.lat_rim)

    def mesh_columns(columns):
        total = own_ref[:, columns] + mm(unpack, back_ref[lat_terms:, columns], TN)
        own_ref[:, columns] = total
        for start, rows in ((0, pl.ds(0, plan.lat_rim)), (plan.lat_rim, last_rim)):
            own_ref[rows, columns] += back_ref[pl.ds(start, plan.lat_rim), columns].astype(
                jnp.float32
            )
        mesh_grad_ref[:, columns] = own_ref[:, columns].astype(jnp.bfloat16)

    column_tiles(plan.width, mesh_columns)


def local(grid_feat, mesh_feat, edges, edge_mask, w_query, w_key, w_value, w_out, cotangent):
    grid_rows, grid_cols, width = grid_feat.shape
    mesh_rows, mesh_cols, _ = mesh_feat.shape
    plan = Plan(
        mesh_rows, mesh_cols, grid_rows, grid_cols, width, lax.axis_size("lat"), lax.axis_size("lon")
    )
    half, full = jnp.bfloat16, jnp.float32
    points, own, nodes = plan.points, plan.own, plan.nodes
    anywhere = pl.BlockSpec(memory_space=pl.ANY)
    vmem = pl.BlockSpec(memory_space=pltpu.VMEM)
    back_rows = 2 * plan.lat_rim + 2 * plan.lon_rim + 4 * plan.corner
    square = (width, width)
    layer_out, grid_grad, mesh_grad = pl.pallas_call(
        functools.partial(layer_kernel, plan),
        out_shape=(
            jax.ShapeDtypeStruct((points, width), half),
            jax.ShapeDtypeStruct((points, width), half),
            jax.ShapeDtypeStruct((own, width), half),
        ),
        in_specs=[anywhere] * 9,
        out_specs=(vmem,) * 3,
        scratch_shapes=[
            pltpu.VMEM((points, width), half),
            pltpu.VMEM((points, width), half),
            pltpu.VMEM(edges.shape, jnp.int32),
            pltpu.VMEM(edges.shape, jnp.int32),
            pltpu.VMEM(square, half),
            pltpu.VMEM(square, half),
            pltpu.VMEM(square, half),
            pltpu.VMEM(square, half),
            pltpu.VMEM((nodes, width), half),
            pltpu.VMEM((2 * plan.lon_rim, width), half),
            pltpu.VMEM((plan.tiles, EDGE_SLOTS, plan.tile_points), jnp.int32),
            pltpu.VMEM((points, width), half),
            pltpu.VMEM((points, width), half),
            pltpu.VMEM((nodes, width), half),
            pltpu.VMEM((nodes, width), half),
            pltpu.VMEM((points, width), half),
            pltpu.VMEM((points, width), half),
            pltpu.VMEM((nodes, width), full),
            pltpu.VMEM((nodes, width), full),
            pltpu.VMEM((plan.keys, plan.tile_points), full),
            pltpu.VMEM((own, width), full),
            pltpu.VMEM((nodes, width), half),
            pltpu.VMEM((back_rows, width), half),
            pltpu.SemaphoreType.DMA((9,)),
            pltpu.SemaphoreType.DMA((8,)),
            pltpu.SemaphoreType.DMA((8,)),
            pltpu.SemaphoreType.DMA((8,)),
            pltpu.SemaphoreType.DMA((8,)),
        ],
        compiler_params=pltpu.CompilerParams(
            collective_id=0, has_side_effects=True, vmem_limit_bytes=52 * 2**20
        ),
        cost_estimate=pl.CostEstimate(
            flops=8 * points * width * width + 8 * nodes * width * width,
            bytes_accessed=8 * width * width + 8 * points * width,
            transcendentals=points * plan.keys * HEAD_COUNT,
        ),
    )(
        grid_feat.reshape(points, width), mesh_feat.reshape(own, width), edges, edge_mask,
        w_query, w_key, w_value, w_out, cotangent.reshape(points, width),
    )
    return (
        layer_out.reshape(grid_feat.shape),
        grid_grad.reshape(grid_feat.shape),
        mesh_grad.reshape(mesh_feat.shape),
    )


def solution(mesh):
    placed = (
        P("lat", "lon", None),
        P("lat", "lon", None),
        P(None, "lat", "lon"),
        P(None, "lat", "lon"),
        P(),
        P(),
        P(),
        P(),
        P("lat", "lon", None),
    )
    return jax.shard_map(
        local,
        mesh=mesh,
        in_specs=placed,
        out_specs=(P("lat", "lon", None), P("lat", "lon", None), P("lat", "lon", None)),
        check_vma=False,
    )
```

time: 69.1 us -> 55.9 us (0.81)
  Pallas kernels: 17.4 us -> 49 us
  starting transfers between devices: 20.4 us -> 0 us
  matrix products: 14 us -> 0 us
  waiting for transfers between devices: 6.5 us -> 0 us
  other arithmetic: 2.97 us -> 0 us
    pallas_call x1, Pallas kernels: 17.4 us -> 49 us  [local(): pl.pallas_call(functools.partial(layer_kernel, plan), out_shape=(jax.Shap...]
    ppermute x8 -> x0, starting transfers between devices: 20.4 us -> none  [shifted(): return lax.ppermute(block, axis, moves)]
    dot_general x8 -> x0, matrix products: 14 us -> none  [mm(): return lax.dot_general(a, b, dims, preferred_element_type=jnp.float32)]
    ppermute x8 -> x0, waiting for transfers between devices: 6.5 us -> none  [shifted(): return lax.ppermute(block, axis, moves)]
    unnamed x22 -> x11, local copies, waits for them, and re-layouts: 1.96 us -> 5.99 us
    slice x4 -> x0, local copies, waits for them, and re-layouts: 2.06 us -> none  [the longest x1 1.83 us: local(): above = shifted(mesh_feat[:reach], 'lat', -1, False)]
    reshape x1 -> x0, local copies, waits for them, and re-layouts: 1.59 us -> none  [local(): targets = edges.reshape(EDGE_SLOTS, points)]
    convert_element_type x3 -> x0, other arithmetic: 1.15 us -> none  [the longest x1 0.76 us: local(): owned.astype(jnp.bfloat16)]
  transfers between devices with their start and end apart: 8 -> 0, of which waited for: 3 -> 0; matrix products, arithmetic and copies ran while one was open for 22% -> 0% of each run, Pallas kernels for 0% -> 0%
where the time goes in v2:
time: 55.9 us; the launch traced here: 55.7 us
  Pallas kernels  49 us (88%)
  local copies, waits for them, and re-layouts  5.99 us (11%)
  between operations  0.66 us (1%)
    pallas_call x1, Pallas kernels, local(): pl.pallas_call(functools.partial(layer_kernel, plan), out_shape=(jax.Shap...  49 us
    unnamed x11, local copies, waits for them, and re-layouts  5.99 us

profile of v2, /device:TPU:0, one launch (start us, length us, event | category | flops | bytes accessed | tf_op | source)
XLA Modules:
  0.0 55.7 jit_solution(16052625352705096044)
XLA Ops:
  0.6 0.0 copy-start
  0.6 0.9 %copy-done = bf16[8,16,1024]{2,1,0:T(8,128)(2,1)S(1)} copy-done((bf16[8,16,1024]{2,1,0:T(8,128)(2,1)S(1)}, bf16[8,16,1024]{2,1,0:T(8,128)(2,1)}, u32[]{:S(2)}) %copy-start) | copy-done | bytes 262168
  1.6 0.0 copy-start.1
  1.6 0.9 %copy-done.1 = s32[12,16,32]{2,1,0:T(8,128)S(1)} copy-done((s32[12,16,32]{2,1,0:T(8,128)S(1)}, s32[12,16,32]{2,1,0:T(8,128)}, u32[]{:S(2)}) %copy-start.1) | copy-done | bytes 24600
  2.5 0.0 copy-start.2
  2.5 0.9 %copy-done.2 = s32[12,16,32]{2,1,0:T(8,128)S(1)} copy-done((s32[12,16,32]{2,1,0:T(8,128)S(1)}, s32[12,16,32]{2,1,0:T(8,128)}, u32[]{:S(2)}) %copy-start.2) | copy-done | bytes 24600
  3.4 49.0 %shard_map.112 = (bf16[512,1024]{1,0:T(8,128)(2,1)S(1)}, bf16[512,1024]{1,0:T(8,128)(2,1)}, bf16[128,1024]{1,0:T(8,128)(2,1)S(1)}) custom-call(bf16[512,1024]{1,0:T(8,128)(2,1)} %bitcast.10, bf16[128,1024]{1,0:T(8,128)(2,1)S(1)} %bitcast.8, s32[12,16,32]{2,1,0:T(8,128)S(1)} %copy-done.1, s32[12,16,32]{2,1,0:T(8,128)S(1)} %copy-done.2, ...), custom_call_target="tpu_custom_call" | custom-call | flops 7516192768 | bytes 12582912 | tf_op jit(solution)/shard_map/pallas_call | solution.py:369
  52.4 0.0 copy-start.3
  52.4 1.0 %copy.15 = bf16[16,32,1024]{2,1,0:T(8,128)(2,1)} copy(bf16[16,32,1024]{2,1,0:T(8,128)(2,1)S(1)} %bitcast.6) | data formatting | bytes 2097152
  53.4 0.6 %copy-done.3 = bf16[512,1024]{1,0:T(8,128)(2,1)S(1)} copy-done((bf16[512,1024]{1,0:T(8,128)(2,1)S(1)}, bf16[512,1024]{1,0:T(8,128)(2,1)}, u32[]{:S(2)}) %copy-start.3) | copy-done | bytes 1048600
  54.0 1.0 %copy.16 = bf16[16,32,1024]{2,1,0:T(8,128)(2,1)} copy(bf16[16,32,1024]{2,1,0:T(8,128)(2,1)S(1)} %bitcast.9) | data formatting | bytes 2097152
  55.0 0.7 %copy.17 = bf16[8,16,1024]{2,1,0:T(8,128)(2,1)} copy(bf16[8,16,1024]{2,1,0:T(8,128)(2,1)S(1)} %bitcast.7) | data formatting | bytes 524288
Async XLA Ops:
  0.6 1.0 %copy-start = (bf16[8,16,1024]{2,1,0:T(8,128)(2,1)S(1)}, bf16[8,16,1024]{2,1,0:T(8,128)(2,1)}, u32[]{:S(2)}) copy-start(bf16[8,16,1024]{2,1,0:T(8,128)(2,1)} %param.10) | copy-start | bytes 786436
  1.6 0.9 %copy-start.1 = (s32[12,16,32]{2,1,0:T(8,128)S(1)}, s32[12,16,32]{2,1,0:T(8,128)}, u32[]{:S(2)}) copy-start(s32[12,16,32]{2,1,0:T(8,128)} %edges_in.1) | copy-start | bytes 73732
  2.5 0.9 %copy-start.2 = (s32[12,16,32]{2,1,0:T(8,128)S(1)}, s32[12,16,32]{2,1,0:T(8,128)}, u32[]{:S(2)}) copy-start(s32[12,16,32]{2,1,0:T(8,128)} %mask_in.1) | copy-start | bytes 73732
  52.4 1.6 %copy-start.3 = (bf16[512,1024]{1,0:T(8,128)(2,1)S(1)}, bf16[512,1024]{1,0:T(8,128)(2,1)}, u32[]{:S(2)}) copy-start(bf16[512,1024]{1,0:T(8,128)(2,1)} %get-tuple-element.7) | copy-start | bytes 3145732

commit v3 on v2

--- a/solution.py
+++ b/solution.py
@@ -13,7 +13,6 @@
 HALO_REACH = 4
 TILE_MESH_ROWS = 2
 ROW_GROUP = 16
-PAIRS_UNROLLED = 4
 NEG_FILL = -1e30
 
 NN = (((1,), (0,)), ((), ()))
@@ -145,7 +144,8 @@
             return jnp.concatenate([block * low, block * high], axis=0)
 
         def joined(both):
-            return jnp.concatenate([both[:head, :tile_points], both[head:, tile_points:]], axis=0).T
+            kept = jnp.concatenate([both[:head, :tile_points], both[head:, tile_points:]], axis=0)
+            return kept.astype(jnp.bfloat16).T
 
         def window_of(ref, lanes):
             return jnp.concatenate([ref[window, lanes] for window, _ in windows], axis=0)
@@ -154,38 +154,39 @@
             for window, first in windows:
                 ref[window, lanes] += block[first : first + window.size]
 
-        def pair_step(index):
-            lanes = pl.ds(pl.multiple_of(index * pair, pair), pair)
+        def first_products(index):
+            lanes = slice(index * pair, (index + 1) * pair)
             q2 = split(q_ref[rows, lanes])
             d2 = split(d_ref[rows, lanes])
             k2 = window_of(k_ref, lanes)
             v2 = window_of(v_ref, lanes)
+            return lanes, q2, d2, k2, v2, mm(k2, q2, NT), mm(v2, d2, NT)
+
+        def rest(lanes, q2, d2, k2, v2, scores, d_prob):
             bias = bias_ref[...]
-            scores = mm(k2, q2, NT) + jnp.concatenate([bias, bias], axis=1)
+            scores = scores + jnp.concatenate([bias, bias], axis=1)
             exps = jnp.exp(scores - jnp.max(scores, axis=0, keepdims=True))
             prob = exps * (1.0 / jnp.sum(exps, axis=0, keepdims=True))
             half = prob.astype(jnp.bfloat16)
-            d_prob = mm(v2, d2, NT)
             centred = jnp.sum(prob * d_prob, axis=0, keepdims=True)
             d_score = (prob * (d_prob - centred)).astype(jnp.bfloat16)
-            att_ref[rows, lanes] = joined(mm(v2, half, TN)).astype(att_ref.dtype)
-            dq_ref[rows, lanes] = (joined(mm(k2, d_score, TN)) * plan.scale).astype(dq_ref.dtype)
+            att_ref[rows, lanes] = joined(mm(v2, half, TN))
+            dq_ref[rows, lanes] = joined(mm(k2, d_score, TN) * plan.scale)
             add_window(dk_ref, lanes, mm(d_score, q2))
             add_window(dv_ref, lanes, mm(half, d2))
 
-        def some_pairs(index, inner):
-            for offset in range(PAIRS_UNROLLED):
-                pair_step(index * PAIRS_UNROLLED + offset)
-            return inner
-
-        lax.fori_loop(0, pairs // PAIRS_UNROLLED, some_pairs, 0)
+        ready = first_products(0)
+        for index in range(pairs):
+            following = first_products(index + 1) if index + 1 < pairs else None
+            rest(*ready)
+            ready = following
         return carry
 
     lax.fori_loop(0, plan.tiles, tile_step, 0)
 
 
 def column_tiles(width, body):
-    tile = min(width, 256)
+    tile = min(width, 512)
 
     def step(index, carry):
         body(pl.ds(pl.multiple_of(index * tile, tile), tile))
@@ -197,11 +198,11 @@
 def layer_kernel(
     plan,
     grid_in, mesh_in, edges_in, mask_in, wq_in, wk_in, wv_in, wo_in, cot_in,
-    out_ref, grid_grad_ref, mesh_grad_ref,
-    grid_ref, cot_ref, edges_ref, mask_ref, wq_ref, wk_ref, wv_ref, wo_ref,
+    out_hbm, grid_grad_hbm, mesh_grad_hbm,
+    out_ref, grid_grad_ref, mesh_grad_ref, grid_ref, cot_ref, edges_ref, mask_ref, wq_ref, wk_ref, wv_ref, wo_ref,
     feat_ref, pack_ref, slot_ref, q_ref, d_ref, k_ref, v_ref, att_ref, dq_ref,
     dk_ref, dv_ref, bias_ref, own_ref, part_ref, back_ref,
-    load_sem, send_sem, recv_sem, back_send_sem, back_recv_sem,
+    load_sem, store_sem, send_sem, recv_sem, back_send_sem, back_recv_sem,
 ):
     reach = HALO_REACH
     lat, lon = lax.axis_index("lat"), lax.axis_index("lon")
@@ -223,19 +224,23 @@
     loads = []
     for index, (source, target) in enumerate(
         (
-            (mesh_in, own_feat), (grid_in, grid_ref), (wq_in, wq_ref), (edges_in, edges_ref),
-            (mask_in, mask_ref), (cot_in, cot_ref), (wo_in, wo_ref), (wk_in, wk_ref),
-            (wv_in, wv_ref),
+            (mesh_in, own_feat), (edges_in, edges_ref), (mask_in, mask_ref), (grid_in, grid_ref),
+            (wq_in, wq_ref), (cot_in, cot_ref), (wo_in, wo_ref), (wk_in, wk_ref), (wv_in, wv_ref),
         )
     ):
         load = pltpu.make_async_copy(source, target, load_sem.at[index])
         load.start()
         loads.append(load)
-    mesh_load, grid_load, wq_load, edges_load, mask_load, cot_load, wo_load, wk_load, wv_load = loads
+    mesh_load, edges_load, mask_load, grid_load, wq_load, cot_load, wo_load, wk_load, wv_load = loads
 
     mesh_load.wait()
     pack = pack_matrix(plan)
     pack_ref[...] = mm(pack, own_feat[...]).astype(jnp.bfloat16)
+    edges_load.wait()
+    mask_load.wait()
+    fill_slots(
+        plan, lat * plan.mesh_rows, lon * plan.mesh_cols, edges_ref, mask_ref, slot_ref
+    )
     pl.semaphore_wait(barrier, len(exchanges))
     corner, lon_rim = plan.corner, plan.lon_rim
     sent = []
@@ -267,11 +272,6 @@
         q_ref[:, columns] = (queries.astype(jnp.float32) * plan.scale).astype(jnp.bfloat16)
 
     column_tiles(plan.width, query_columns)
-    edges_load.wait()
-    mask_load.wait()
-    fill_slots(
-        plan, lat * plan.mesh_rows, lon * plan.mesh_cols, edges_ref, mask_ref, slot_ref
-    )
     cot_load.wait()
     wo_load.wait()
 
@@ -332,6 +332,13 @@
         grid_grad_ref[:, columns] = grad.astype(jnp.bfloat16)
 
     column_tiles(plan.width, out_columns)
+    stores = [
+        pltpu.make_async_copy(out_ref, out_hbm, store_sem.at[0]),
+        pltpu.make_async_copy(grid_grad_ref, grid_grad_hbm, store_sem.at[1]),
+        pltpu.make_async_copy(mesh_grad_ref, mesh_grad_hbm, store_sem.at[2]),
+    ]
+    stores[0].start()
+    stores[1].start()
     for copy in returned:
         copy.wait()
     corners = [
@@ -352,6 +359,22 @@
         mesh_grad_ref[:, columns] = own_ref[:, columns].astype(jnp.bfloat16)
 
     column_tiles(plan.width, mesh_columns)
+    stores[2].start()
+    for store in stores:
+        store.wait()
+
+
+def store_kernel(out_in, grid_grad_in, mesh_grad_in, out_ref, grid_grad_ref, mesh_grad_ref, sem):
+    copies = [
+        pltpu.make_async_copy(source, target, sem.at[index])
+        for index, (source, target) in enumerate(
+            ((out_in, out_ref), (grid_grad_in, grid_grad_ref), (mesh_grad_in, mesh_grad_ref))
+        )
+    ]
+    for copy in copies:
+        copy.start()
+    for copy in copies:
+        copy.wait()
 
 
 def local(grid_feat, mesh_feat, edges, edge_mask, w_query, w_key, w_value, w_out, cotangent):
@@ -363,7 +386,7 @@
     half, full = jnp.bfloat16, jnp.float32
     points, own, nodes = plan.points, plan.own, plan.nodes
     anywhere = pl.BlockSpec(memory_space=pl.ANY)
-    vmem = pl.BlockSpec(memory_space=pltpu.VMEM)
+    hbm = pl.BlockSpec(memory_space=pltpu.HBM)
     back_rows = 2 * plan.lat_rim + 2 * plan.lon_rim + 4 * plan.corner
     square = (width, width)
     layer_out, grid_grad, mesh_grad = pl.pallas_call(
@@ -373,9 +396,12 @@
             jax.ShapeDtypeStruct((points, width), half),
             jax.ShapeDtypeStruct((own, width), half),
         ),
-        in_specs=[anywhere] * 9,
-        out_specs=(vmem,) * 3,
+        in_specs=[hbm] * 9,
+        out_specs=(hbm,) * 3,
         scratch_shapes=[
+            pltpu.VMEM((points, width), half),
+            pltpu.VMEM((points, width), half),
+            pltpu.VMEM((own, width), half),
             pltpu.VMEM((points, width), half),
             pltpu.VMEM((points, width), half),
             pltpu.VMEM(edges.shape, jnp.int32),
@@ -400,13 +426,14 @@
             pltpu.VMEM((nodes, width), half),
             pltpu.VMEM((back_rows, width), half),
             pltpu.SemaphoreType.DMA((9,)),
+            pltpu.SemaphoreType.DMA((3,)),
             pltpu.SemaphoreType.DMA((8,)),
             pltpu.SemaphoreType.DMA((8,)),
             pltpu.SemaphoreType.DMA((8,)),
             pltpu.SemaphoreType.DMA((8,)),
         ],
         compiler_params=pltpu.CompilerParams(
-            collective_id=0, has_side_effects=True, vmem_limit_bytes=52 * 2**20
+            collective_id=0, has_side_effects=True, vmem_limit_bytes=64 * 2**20
         ),
         cost_estimate=pl.CostEstimate(
             flops=8 * points * width * width + 8 * nodes * width * width,
@@ -417,6 +444,15 @@
         grid_feat.reshape(points, width), mesh_feat.reshape(own, width), edges, edge_mask,
         w_query, w_key, w_value, w_out, cotangent.reshape(points, width),
     )
+    results = (layer_out, grid_grad, mesh_grad)
+    layer_out, grid_grad, mesh_grad = pl.pallas_call(
+        store_kernel,
+        out_shape=tuple(jax.ShapeDtypeStruct(x.shape, x.dtype) for x in results),
+        in_specs=[anywhere] * 3,
+        out_specs=(hbm,) * 3,
+        scratch_shapes=[pltpu.SemaphoreType.DMA((3,))],
+        compiler_params=pltpu.CompilerParams(vmem_limit_bytes=64 * 2**20),
+    )(*results)
     return (
         layer_out.reshape(grid_feat.shape),
         grid_grad.reshape(grid_feat.shape),

time: 55.9 us -> 121 us (2.16)
  Pallas kernels: 49 us -> 121 us
  local copies, waits for them, and re-layouts: 5.99 us -> 0 us
    pallas_call x0 -> x1, Pallas kernels: none -> 72.6 us  [local(): pl.pallas_call(store_kernel, out_shape=tuple((jax.ShapeDtypeStruct(x.shap...]
    unnamed x11 -> x0, local copies, waits for them, and re-layouts: 5.99 us -> none
where the time goes in v3:
time: 121 us
  Pallas kernels  121 us (100%)
    pallas_call x1, Pallas kernels, local(): pl.pallas_call(store_kernel, out_shape=tuple((jax.ShapeDtypeStruct(x.shap...  72.6 us
    pallas_call x1, Pallas kernels, local(): pl.pallas_call(functools.partial(layer_kernel, plan), out_shape=(jax.Shap...  48 us

profile of v3, /device:TPU:0, one launch (start us, length us, event | category | flops | bytes accessed | tf_op | source)
XLA Modules:
  0.0 121.3 jit_solution(5712822470878562406)
XLA Ops:
  0.6 48.0 %shard_map.112 = (bf16[512,1024]{1,0:T(8,128)(2,1)}, bf16[512,1024]{1,0:T(8,128)(2,1)}, bf16[128,1024]{1,0:T(8,128)(2,1)}) custom-call(bf16[512,1024]{1,0:T(8,128)(2,1)} %bitcast.6, bf16[128,1024]{1,0:T(8,128)(2,1)} %bitcast.10, s32[12,16,32]{2,1,0:T(8,128)} %edges_in.1, s32[12,16,32]{2,1,0:T(8,128)} %mask_in.1, bf16[1024,1024]{1,0:T(8,128)(2,1)} %wq_in.1, ...), custom_call_target="tpu_custom_call" | custom-call | flops 7516192768 | bytes 12582912 | tf_op jit(solution)/shard_map/pallas_call | solution.py:392
  48.7 72.6 %shard_map.113 = (bf16[512,1024]{1,0:T(8,128)(2,1)}, bf16[512,1024]{1,0:T(8,128)(2,1)}, bf16[128,1024]{1,0:T(8,128)(2,1)}) custom-call(bf16[512,1024]{1,0:T(8,128)(2,1)} %get-tuple-element.9.out_in, bf16[512,1024]{1,0:T(8,128)(2,1)} %get-tuple-element.10.grid_grad_in, bf16[128,1024]{1,0:T(8,128)(2,1)} %get-tuple-element.11.mesh_grad_in), custom_call_target="tpu_custom_call" | custom-call | tf_op jit(solution)/shard_map/pallas_call | solution.py:448

commit v4 on v3

--- a/solution.py
+++ b/solution.py
@@ -53,6 +53,17 @@
         self.side_keys = min(self.strip, -(-covered // ROW_GROUP) * ROW_GROUP)
         self.keys = self.mid_keys + 2 * self.side_keys
 
+        self.early = (mesh_rows - reach) // TILE_MESH_ROWS
+
+    def node_ranges(self, low, high):
+        reach, cols = HALO_REACH, self.mesh_cols
+        right = self.mid + self.strip
+        return (
+            slice(low * cols, high * cols),
+            slice(self.mid + low * reach, self.mid + high * reach),
+            slice(right + low * reach, right + high * reach),
+        )
+
     def side_start(self, tile):
         return (tile * self.side_step) // ROW_GROUP * ROW_GROUP
 
@@ -62,12 +73,12 @@
         left, right = mid, mid + strip
         return (
             (-1, 0, 0, lat_rim),
-            (1, 0, mid - lat_rim, lat_rim),
+            (-1, -1, left, corner),
+            (-1, 1, right, corner),
             (0, -1, left + corner, lon_rim),
             (0, 1, right + corner, lon_rim),
-            (-1, -1, left, corner),
+            (1, 0, mid - lat_rim, lat_rim),
             (1, -1, left + strip - corner, corner),
-            (-1, 1, right, corner),
             (1, 1, right + strip - corner, corner),
         )
 
@@ -111,7 +122,8 @@
 
 
 def attend_tiles(
-    plan, slot_ref, q_ref, d_ref, k_ref, v_ref, att_ref, dq_ref, dk_ref, dv_ref, bias_ref
+    plan, slot_ref, q_ref, d_ref, k_ref, v_ref, att_ref, dq_ref, dk_ref, dv_ref, bias_ref,
+    at_middle,
 ):
     head, tile_points = plan.head, plan.tile_points
     pair = 2 * head
@@ -123,6 +135,7 @@
     dv_ref[...] = jnp.zeros_like(dv_ref)
 
     def tile_step(tile, carry):
+        pl.when(tile == plan.early)(at_middle)
         rows = pl.ds(pl.multiple_of(tile * tile_points, tile_points), tile_points)
         side = plan.side_start(tile)
         windows = (
@@ -201,7 +214,7 @@
     out_hbm, grid_grad_hbm, mesh_grad_hbm,
     out_ref, grid_grad_ref, mesh_grad_ref, grid_ref, cot_ref, edges_ref, mask_ref, wq_ref, wk_ref, wv_ref, wo_ref,
     feat_ref, pack_ref, slot_ref, q_ref, d_ref, k_ref, v_ref, att_ref, dq_ref,
-    dk_ref, dv_ref, bias_ref, own_ref, part_ref, back_ref,
+    dk_ref, dv_ref, dk_half_ref, dv_half_ref, bias_ref, own_ref, part_ref, back_ref,
     load_sem, store_sem, send_sem, recv_sem, back_send_sem, back_recv_sem,
 ):
     reach = HALO_REACH
@@ -261,8 +274,10 @@
             device_id=device(-lat_step, -lon_step),
             device_id_type=pl.DeviceIdType.MESH,
         )
+        sent.append(copy)
+    above, beside, below = sent[:3], sent[3:5], sent[5:]
+    for copy in above + beside:
         copy.start()
-        sent.append(copy)
 
     grid_load.wait()
     wq_load.wait()
@@ -281,27 +296,45 @@
     column_tiles(plan.width, d_columns)
     wk_load.wait()
     wv_load.wait()
-    for copy in sent:
-        copy.wait()
-
-    def pair_columns(columns):
-        feat = feat_ref[...]
-        k_ref[:, columns] = mm(feat, wk_ref[:, columns]).astype(jnp.bfloat16)
-        v_ref[:, columns] = mm(feat, wv_ref[:, columns]).astype(jnp.bfloat16)
-
-    column_tiles(plan.width, pair_columns)
-    attend_tiles(
-        plan, slot_ref, q_ref, d_ref, k_ref, v_ref, att_ref, dq_ref, dk_ref, dv_ref, bias_ref
-    )
-    k_ref[...] = dk_ref[...].astype(jnp.bfloat16)
-    v_ref[...] = dv_ref[...].astype(jnp.bfloat16)
-
-    def part_columns(columns):
-        part = mm(k_ref[...], wk_ref[columns, :], NT) + mm(v_ref[...], wv_ref[columns, :], NT)
-        part_ref[:, columns] = part.astype(jnp.bfloat16)
-        own_ref[:, columns] = part[first_own : first_own + plan.own]
-
-    column_tiles(plan.width, part_columns)
+    for copy in below:
+        copy.start()
+
+    def project(low, high):
+        ranges = plan.node_ranges(low, high)
+
+        def pair_columns(columns):
+            feat = jnp.concatenate([feat_ref[nodes, :] for nodes in ranges], axis=0)
+            for weight_ref, target_ref in ((wk_ref, k_ref), (wv_ref, v_ref)):
+                rows = mm(feat, weight_ref[:, columns]).astype(jnp.bfloat16)
+                first = 0
+                for nodes in ranges:
+                    count = nodes.stop - nodes.start
+                    target_ref[nodes, columns] = rows[first : first + count]
+                    first += count
+
+        column_tiles(plan.width, pair_columns)
+
+    def project_gradients(low, high):
+        ranges = plan.node_ranges(low, high)
+        for nodes in ranges:
+            dk_half_ref[nodes, :] = dk_ref[nodes, :].astype(jnp.bfloat16)
+            dv_half_ref[nodes, :] = dv_ref[nodes, :].astype(jnp.bfloat16)
+
+        def part_columns(columns):
+            d_keys = jnp.concatenate([dk_half_ref[nodes, :] for nodes in ranges], axis=0)
+            d_values = jnp.concatenate([dv_half_ref[nodes, :] for nodes in ranges], axis=0)
+            part = mm(d_keys, wk_ref[columns, :], NT) + mm(d_values, wv_ref[columns, :], NT)
+            if low > 0:
+                own_ref[:, columns] = part[: plan.own]
+            part = part.astype(jnp.bfloat16)
+            first = 0
+            for nodes in ranges:
+                count = nodes.stop - nodes.start
+                part_ref[nodes, columns] = part[first : first + count]
+                first += count
+
+        column_tiles(plan.width, part_columns)
+
     returned = []
     for index, (lat_step, lon_step, first, count) in enumerate(exchanges):
         if lon_step == 0:
@@ -322,8 +355,28 @@
             device_id=device(lat_step, lon_step),
             device_id_type=pl.DeviceIdType.MESH,
         )
+        returned.append(copy)
+
+    padded_rows = plan.mesh_rows + 2 * reach
+
+    def at_middle():
+        for copy in below:
+            copy.wait()
+        project(plan.mesh_rows + reach, padded_rows)
+        project_gradients(0, reach)
+        for copy in returned[:3]:
+            copy.start()
+
+    for copy in above + beside:
+        copy.wait()
+    project(0, plan.mesh_rows + reach)
+    attend_tiles(
+        plan, slot_ref, q_ref, d_ref, k_ref, v_ref, att_ref, dq_ref, dk_ref, dv_ref, bias_ref,
+        at_middle,
+    )
+    project_gradients(reach, padded_rows)
+    for copy in returned[3:]:
         copy.start()
-        returned.append(copy)
 
     def out_columns(columns):
         out = grid_ref[:, columns].astype(jnp.float32) + mm(att_ref[...], wo_ref[:, columns])
@@ -364,17 +417,27 @@
         store.wait()
 
 
-def store_kernel(out_in, grid_grad_in, mesh_grad_in, out_ref, grid_grad_ref, mesh_grad_ref, sem):
-    copies = [
-        pltpu.make_async_copy(source, target, sem.at[index])
-        for index, (source, target) in enumerate(
-            ((out_in, out_ref), (grid_grad_in, grid_grad_ref), (mesh_grad_in, mesh_grad_ref))
-        )
-    ]
-    for copy in copies:
-        copy.start()
-    for copy in copies:
-        copy.wait()
+def store_kernel(rows, *refs):
+    sources, targets, held = refs[:3], refs[3:6], refs[6:9]
+    load_sem, store_sem = refs[9:]
+    loads, stores = [], []
+    for source, target, buffer in zip(sources, targets, held):
+        for start in range(0, source.shape[0], rows):
+            part = pl.ds(start, rows)
+            index = len(loads)
+            loads.append(
+                pltpu.make_async_copy(source.at[part], buffer.at[part], load_sem.at[index])
+            )
+            stores.append(
+                pltpu.make_async_copy(buffer.at[part], target.at[part], store_sem.at[index])
+            )
+    for load in loads:
+        load.start()
+    for load, store in zip(loads, stores):
+        load.wait()
+        store.start()
+    for store in stores:
+        store.wait()
 
 
 def local(grid_feat, mesh_feat, edges, edge_mask, w_query, w_key, w_value, w_out, cotangent):
@@ -421,6 +484,8 @@
             pltpu.VMEM((points, width), half),
             pltpu.VMEM((nodes, width), full),
             pltpu.VMEM((nodes, width), full),
+            pltpu.VMEM((nodes, width), half),
+            pltpu.VMEM((nodes, width), half),
             pltpu.VMEM((plan.keys, plan.tile_points), full),
             pltpu.VMEM((own, width), full),
             pltpu.VMEM((nodes, width), half),
@@ -446,11 +511,12 @@
     )
     results = (layer_out, grid_grad, mesh_grad)
     layer_out, grid_grad, mesh_grad = pl.pallas_call(
-        store_kernel,
+        functools.partial(store_kernel, own),
         out_shape=tuple(jax.ShapeDtypeStruct(x.shape, x.dtype) for x in results),
         in_specs=[anywhere] * 3,
         out_specs=(hbm,) * 3,
-        scratch_shapes=[pltpu.SemaphoreType.DMA((3,))],
+        scratch_shapes=[pltpu.VMEM(x.shape, x.dtype) for x in results]
+        + [pltpu.SemaphoreType.DMA((2 * points // own + 1,))] * 2,
         compiler_params=pltpu.CompilerParams(vmem_limit_bytes=64 * 2**20),
     )(*results)
     return (

time: 121 us -> 45.7 us (0.38)
  Pallas kernels: 121 us -> 44.9 us
    pallas_call x1, Pallas kernels: 72.6 us -> 2.5 us  [local(): pl.pallas_call(functools.partial(store_kernel, own), out_shape=tuple((jax...]
    pallas_call x1, Pallas kernels: 48 us -> 42.4 us  [local(): pl.pallas_call(functools.partial(layer_kernel, plan), out_shape=(jax.Shap...]
where the time goes in v4:
time: 45.7 us; the launch traced here: 45.5 us
  Pallas kernels  44.9 us (98%)
  between operations  0.64 us (1%)
    pallas_call x1, Pallas kernels, local(): pl.pallas_call(functools.partial(layer_kernel, plan), out_shape=(jax.Shap...  42.4 us
    pallas_call x1, Pallas kernels, local(): pl.pallas_call(functools.partial(store_kernel, own), out_shape=tuple((jax...  2.5 us

profile of v4, /device:TPU:0, one launch (start us, length us, event | category | flops | bytes accessed | tf_op | source)
XLA Modules:
  0.0 45.5 jit_solution(599942017347914034)
XLA Ops:
  0.6 42.4 %shard_map.112 = (bf16[512,1024]{1,0:T(8,128)(2,1)}, bf16[512,1024]{1,0:T(8,128)(2,1)}, bf16[128,1024]{1,0:T(8,128)(2,1)}) custom-call(bf16[512,1024]{1,0:T(8,128)(2,1)} %bitcast.6, bf16[128,1024]{1,0:T(8,128)(2,1)} %bitcast.10, s32[12,16,32]{2,1,0:T(8,128)} %edges_in.1, s32[12,16,32]{2,1,0:T(8,128)} %mask_in.1, bf16[1024,1024]{1,0:T(8,128)(2,1)} %wq_in.1, ...), custom_call_target="tpu_custom_call" | custom-call | flops 7516192768 | bytes 12582912 | tf_op jit(solution)/shard_map/pallas_call | solution.py:455
  43.0 2.5 %shard_map.113 = (bf16[512,1024]{1,0:T(8,128)(2,1)}, bf16[512,1024]{1,0:T(8,128)(2,1)}, bf16[128,1024]{1,0:T(8,128)(2,1)}) custom-call(bf16[512,1024]{1,0:T(8,128)(2,1)} %get-tuple-element.9.refs_0_, bf16[512,1024]{1,0:T(8,128)(2,1)} %get-tuple-element.10.refs_1_, bf16[128,1024]{1,0:T(8,128)(2,1)} %get-tuple-element.11.refs_2_), custom_call_target="tpu_custom_call" | custom-call | tf_op jit(solution)/shard_map/pallas_call | solution.py:513

commit v5 on v4

--- a/solution.py
+++ b/solution.py
@@ -11,7 +11,7 @@
 HEAD_COUNT = 16
 EDGE_SLOTS = 12
 HALO_REACH = 4
-TILE_MESH_ROWS = 2
+TILE_MESH_ROWS = 4
 ROW_GROUP = 16
 NEG_FILL = -1e30
 
@@ -41,19 +41,19 @@
         self.lat_rim = reach * mesh_cols
         self.lon_rim = mesh_rows * reach
         self.corner = reach * reach
-        self.tiles = mesh_rows // TILE_MESH_ROWS
-        self.tile_grid_rows = grid_rows // self.tiles
-        self.tile_points = self.tile_grid_rows * grid_cols
-        window_rows = TILE_MESH_ROWS + 2 * reach
-        self.mid_step = TILE_MESH_ROWS * mesh_cols
-        self.mid_keys = window_rows * mesh_cols
-        self.side_step = TILE_MESH_ROWS * reach
-        slack = max((tile * self.side_step) % ROW_GROUP for tile in range(self.tiles))
-        covered = window_rows * reach + slack
-        self.side_keys = min(self.strip, -(-covered // ROW_GROUP) * ROW_GROUP)
-        self.keys = self.mid_keys + 2 * self.side_keys
-
-        self.early = (mesh_rows - reach) // TILE_MESH_ROWS
+        self.block_cols = 2 * reach
+        self.blocks = (mesh_cols + 2 * reach) // self.block_cols
+        self.block = padded_rows * self.block_cols
+        self.col_tiles = mesh_cols // self.block_cols
+        self.row_tiles = mesh_rows // TILE_MESH_ROWS
+        self.tiles = self.row_tiles * self.col_tiles
+        self.tile_grid_rows = grid_rows // self.row_tiles
+        self.tile_grid_cols = grid_cols // self.col_tiles
+        self.tile_points = self.tile_grid_rows * self.tile_grid_cols
+        self.row_step = TILE_MESH_ROWS * self.block_cols
+        self.side_keys = (TILE_MESH_ROWS + 2 * reach) * self.block_cols
+        self.keys = 2 * self.side_keys
+        self.early = (mesh_rows - reach) // TILE_MESH_ROWS * self.col_tiles
 
     def node_ranges(self, low, high):
         reach, cols = HALO_REACH, self.mesh_cols
@@ -64,8 +64,14 @@
             slice(right + low * reach, right + high * reach),
         )
 
-    def side_start(self, tile):
-        return (tile * self.side_step) // ROW_GROUP * ROW_GROUP
+    def block_ranges(self, low, high):
+        return tuple(
+            slice(
+                block * self.block + low * self.block_cols,
+                block * self.block + high * self.block_cols,
+            )
+            for block in range(self.blocks)
+        )
 
     def exchanges(self):
         mid, strip = self.mid, self.strip
@@ -95,13 +101,34 @@
     return hit.astype(jnp.float32).astype(jnp.bfloat16)
 
 
+def block_permutation(plan, rows, to_blocks):
+    reach, cols, wide = HALO_REACH, plan.mesh_cols, plan.block_cols
+    count = rows * (cols + 2 * reach)
+    vector = (count, 1) if to_blocks else (1, count)
+    node = lax.broadcasted_iota(jnp.int32, vector, 0 if to_blocks else 1)
+    block = jnp.zeros_like(node)
+    for edge in range(1, plan.blocks):
+        block = block + (node >= edge * rows * wide).astype(jnp.int32)
+    within = node - block * (rows * wide)
+    row = within // wide
+    col = within - row * wide + block * wide
+    left = rows * cols + row * reach + col
+    middle = row * cols + col - reach
+    right = left + rows * reach - reach - cols
+    place = jnp.where(col < reach, left, jnp.where(col < reach + cols, middle, right))
+    other = lax.broadcasted_iota(jnp.int32, (count, count), 1 if to_blocks else 0)
+    return (other == place).astype(jnp.float32).astype(jnp.bfloat16)
+
+
 def fill_slots(plan, lat_start, lon_start, edges_ref, mask_ref, slot_ref):
-    reach, cols = HALO_REACH, plan.mesh_cols
+    reach, wide = HALO_REACH, plan.block_cols
     lon_total = plan.mesh_cols * plan.lon_count
     for tile in range(plan.tiles):
-        rows = range(tile * plan.tile_grid_rows, (tile + 1) * plan.tile_grid_rows)
-        target = jnp.concatenate([edges_ref[:, row, :] for row in rows], axis=1)
-        live = jnp.concatenate([mask_ref[:, row, :] for row in rows], axis=1)
+        row_tile, col_tile = divmod(tile, plan.col_tiles)
+        rows = range(row_tile * plan.tile_grid_rows, (row_tile + 1) * plan.tile_grid_rows)
+        cols = slice(col_tile * plan.tile_grid_cols, (col_tile + 1) * plan.tile_grid_cols)
+        target = jnp.concatenate([edges_ref[:, row, cols] for row in rows], axis=1)
+        live = jnp.concatenate([mask_ref[:, row, cols] for row in rows], axis=1)
         if lon_total & (lon_total - 1):
             node_row = lax.div(target, jnp.full_like(target, lon_total))
         else:
@@ -111,13 +138,10 @@
         node_col = target - node_row * lon_total - lon_start + reach
         node_col = jnp.where(node_col < 0, node_col + lon_total, node_col)
         node_col = jnp.where(node_col >= lon_total, node_col - lon_total, node_col)
-        node_row = node_row - lat_start + reach
-        side = plan.mid_keys + node_row * reach - plan.side_start(tile)
-        middle = node_row * cols + node_col - reach - tile * plan.mid_step
-        right = side + plan.side_keys + node_col - cols - reach
-        slot = jnp.where(
-            node_col < reach, side + node_col, jnp.where(node_col < cols + reach, middle, right)
-        )
+        node_row = node_row - lat_start + reach - row_tile * TILE_MESH_ROWS
+        node_col = node_col - col_tile * wide
+        first = node_row * wide + node_col
+        slot = jnp.where(node_col < wide, first, first + (plan.side_keys - wide))
         slot_ref[tile] = jnp.where(live > 0, slot, -1)
 
 
@@ -136,15 +160,23 @@
 
     def tile_step(tile, carry):
         pl.when(tile == plan.early)(at_middle)
-        rows = pl.ds(pl.multiple_of(tile * tile_points, tile_points), tile_points)
-        side = plan.side_start(tile)
-        windows = (
-            (pl.ds(pl.multiple_of(tile * plan.mid_step, ROW_GROUP), plan.mid_keys), 0),
-            (pl.ds(pl.multiple_of(plan.mid + side, ROW_GROUP), plan.side_keys), plan.mid_keys),
+        row_tile, col_tile = tile // plan.col_tiles, tile % plan.col_tiles
+        first_point = (
+            row_tile * (plan.tile_grid_rows * plan.grid_cols) + col_tile * plan.tile_grid_cols
+        )
+        segments = tuple(
+            pl.ds(
+                pl.multiple_of(first_point + row * plan.grid_cols, ROW_GROUP), plan.tile_grid_cols
+            )
+            for row in range(plan.tile_grid_rows)
+        )
+        first_key = col_tile * plan.block + row_tile * plan.row_step
+        windows = tuple(
             (
-                pl.ds(pl.multiple_of(plan.mid + plan.strip + side, ROW_GROUP), plan.side_keys),
-                plan.mid_keys + plan.side_keys,
-            ),
+                pl.ds(pl.multiple_of(first_key + side * plan.block, ROW_GROUP), plan.side_keys),
+                side * plan.side_keys,
+            )
+            for side in range(2)
         )
         key_id = lax.broadcasted_iota(jnp.int32, (plan.keys, tile_points), 0)
         slots = slot_ref[tile]
@@ -160,6 +192,14 @@
             kept = jnp.concatenate([both[:head, :tile_points], both[head:, tile_points:]], axis=0)
             return kept.astype(jnp.bfloat16).T
 
+        def points_of(ref, lanes):
+            return jnp.concatenate([ref[segment, lanes] for segment in segments], axis=0)
+
+        def put_points(ref, lanes, block):
+            wide = plan.tile_grid_cols
+            for row, segment in enumerate(segments):
+                ref[segment, lanes] = block[row * wide : (row + 1) * wide]
+
         def window_of(ref, lanes):
             return jnp.concatenate([ref[window, lanes] for window, _ in windows], axis=0)
 
@@ -169,8 +209,8 @@
 
         def first_products(index):
             lanes = slice(index * pair, (index + 1) * pair)
-            q2 = split(q_ref[rows, lanes])
-            d2 = split(d_ref[rows, lanes])
+            q2 = split(points_of(q_ref, lanes))
+            d2 = split(points_of(d_ref, lanes))
             k2 = window_of(k_ref, lanes)
             v2 = window_of(v_ref, lanes)
             return lanes, q2, d2, k2, v2, mm(k2, q2, NT), mm(v2, d2, NT)
@@ -183,8 +223,8 @@
             half = prob.astype(jnp.bfloat16)
             centred = jnp.sum(prob * d_prob, axis=0, keepdims=True)
             d_score = (prob * (d_prob - centred)).astype(jnp.bfloat16)
-            att_ref[rows, lanes] = joined(mm(v2, half, TN))
-            dq_ref[rows, lanes] = joined(mm(k2, d_score, TN) * plan.scale)
+            put_points(att_ref, lanes, joined(mm(v2, half, TN)))
+            put_points(dq_ref, lanes, joined(mm(k2, d_score, TN) * plan.scale))
             add_window(dk_ref, lanes, mm(d_score, q2))
             add_window(dv_ref, lanes, mm(half, d2))
 
@@ -300,38 +340,45 @@
         copy.start()
 
     def project(low, high):
-        ranges = plan.node_ranges(low, high)
+        ranges = plan.block_ranges(low, high)
+        feat = jnp.concatenate([feat_ref[nodes, :] for nodes in plan.node_ranges(low, high)], axis=0)
+        count = feat.shape[0]
+        to_blocks = block_permutation(plan, high - low, True)
+        dk_half_ref[0:count, :] = mm(to_blocks, feat).astype(jnp.bfloat16)
 
         def pair_columns(columns):
-            feat = jnp.concatenate([feat_ref[nodes, :] for nodes in ranges], axis=0)
+            feat = dk_half_ref[0:count, :]
             for weight_ref, target_ref in ((wk_ref, k_ref), (wv_ref, v_ref)):
                 rows = mm(feat, weight_ref[:, columns]).astype(jnp.bfloat16)
                 first = 0
                 for nodes in ranges:
-                    count = nodes.stop - nodes.start
-                    target_ref[nodes, columns] = rows[first : first + count]
-                    first += count
+                    size = nodes.stop - nodes.start
+                    target_ref[nodes, columns] = rows[first : first + size]
+                    first += size
 
         column_tiles(plan.width, pair_columns)
 
     def project_gradients(low, high):
         ranges = plan.node_ranges(low, high)
-        for nodes in ranges:
-            dk_half_ref[nodes, :] = dk_ref[nodes, :].astype(jnp.bfloat16)
-            dv_half_ref[nodes, :] = dv_ref[nodes, :].astype(jnp.bfloat16)
+        from_blocks = block_permutation(plan, high - low, False)
+        count = from_blocks.shape[0]
+        for source_ref, half_ref in ((dk_ref, dk_half_ref), (dv_ref, dv_half_ref)):
+            terms = jnp.concatenate(
+                [source_ref[nodes, :] for nodes in plan.block_ranges(low, high)], axis=0
+            )
+            half_ref[0:count, :] = mm(from_blocks, terms.astype(jnp.bfloat16)).astype(jnp.bfloat16)
 
         def part_columns(columns):
-            d_keys = jnp.concatenate([dk_half_ref[nodes, :] for nodes in ranges], axis=0)
-            d_values = jnp.concatenate([dv_half_ref[nodes, :] for nodes in ranges], axis=0)
-            part = mm(d_keys, wk_ref[columns, :], NT) + mm(d_values, wv_ref[columns, :], NT)
+            part = mm(dk_half_ref[0:count, :], wk_ref[columns, :], NT)
+            part = part + mm(dv_half_ref[0:count, :], wv_ref[columns, :], NT)
             if low > 0:
                 own_ref[:, columns] = part[: plan.own]
             part = part.astype(jnp.bfloat16)
             first = 0
             for nodes in ranges:
-                count = nodes.stop - nodes.start
-                part_ref[nodes, columns] = part[first : first + count]
-                first += count
+                size = nodes.stop - nodes.start
+                part_ref[nodes, columns] = part[first : first + size]
+                first += size
 
         column_tiles(plan.width, part_columns)
 

time: 45.7 us -> 45 us (0.985)
  Pallas kernels: 44.9 us -> 44.2 us
    pallas_call x1, Pallas kernels: 42.4 us -> 41.7 us  [local(): pl.pallas_call(functools.partial(layer_kernel, plan), out_shape=(jax.Shap...]
where the time goes in v5:
time: 45 us; the launch traced here: 44.8 us
  Pallas kernels  44.2 us (98%)
  between operations  0.64 us (1%)
    pallas_call x1, Pallas kernels, local(): pl.pallas_call(functools.partial(layer_kernel, plan), out_shape=(jax.Shap...  41.7 us
    pallas_call x1, Pallas kernels, local(): pl.pallas_call(functools.partial(store_kernel, own), out_shape=tuple((jax...  2.5 us

profile of v5, /device:TPU:0, one launch (start us, length us, event | category | flops | bytes accessed | tf_op | source)
XLA Modules:
  0.0 44.8 jit_solution(2486165530758367343)
XLA Ops:
  0.6 41.7 %shard_map.112 = (bf16[512,1024]{1,0:T(8,128)(2,1)}, bf16[512,1024]{1,0:T(8,128)(2,1)}, bf16[128,1024]{1,0:T(8,128)(2,1)}) custom-call(bf16[512,1024]{1,0:T(8,128)(2,1)} %bitcast.6, bf16[128,1024]{1,0:T(8,128)(2,1)} %bitcast.10, s32[12,16,32]{2,1,0:T(8,128)} %edges_in.1, s32[12,16,32]{2,1,0:T(8,128)} %mask_in.1, bf16[1024,1024]{1,0:T(8,128)(2,1)} %wq_in.1, ...), custom_call_target="tpu_custom_call" | custom-call | flops 7516192768 | bytes 12582912 | tf_op jit(solution)/shard_map/pallas_call | solution.py:502
  42.3 2.5 %shard_map.113 = (bf16[512,1024]{1,0:T(8,128)(2,1)}, bf16[512,1024]{1,0:T(8,128)(2,1)}, bf16[128,1024]{1,0:T(8,128)(2,1)}) custom-call(bf16[512,1024]{1,0:T(8,128)(2,1)} %get-tuple-element.9.refs_0_, bf16[512,1024]{1,0:T(8,128)(2,1)} %get-tuple-element.10.refs_1_, bf16[128,1024]{1,0:T(8,128)(2,1)} %get-tuple-element.11.refs_2_), custom_call_target="tpu_custom_call" | custom-call | tf_op jit(solution)/shard_map/pallas_call | solution.py:560

commit v6 on v5

--- a/solution.py
+++ b/solution.py
@@ -123,26 +123,28 @@
 def fill_slots(plan, lat_start, lon_start, edges_ref, mask_ref, slot_ref):
     reach, wide = HALO_REACH, plan.block_cols
     lon_total = plan.mesh_cols * plan.lon_count
+    target = edges_ref[...]
+    row_tile = lax.broadcasted_iota(jnp.int32, target.shape, 1) // plan.tile_grid_rows
+    col_tile = lax.broadcasted_iota(jnp.int32, target.shape, 2) // plan.tile_grid_cols
+    if lon_total & (lon_total - 1):
+        node_row = lax.div(target, jnp.full_like(target, lon_total))
+    else:
+        node_row = lax.shift_right_logical(
+            target, jnp.full_like(target, lon_total.bit_length() - 1)
+        )
+    node_col = target - node_row * lon_total - lon_start + reach
+    node_col = jnp.where(node_col < 0, node_col + lon_total, node_col)
+    node_col = jnp.where(node_col >= lon_total, node_col - lon_total, node_col)
+    node_row = node_row - lat_start + reach - row_tile * TILE_MESH_ROWS
+    node_col = node_col - col_tile * wide
+    first = node_row * wide + node_col
+    slots = jnp.where(node_col < wide, first, first + (plan.side_keys - wide))
+    slots = jnp.where(mask_ref[...] > 0, slots, -1)
     for tile in range(plan.tiles):
-        row_tile, col_tile = divmod(tile, plan.col_tiles)
-        rows = range(row_tile * plan.tile_grid_rows, (row_tile + 1) * plan.tile_grid_rows)
-        cols = slice(col_tile * plan.tile_grid_cols, (col_tile + 1) * plan.tile_grid_cols)
-        target = jnp.concatenate([edges_ref[:, row, cols] for row in rows], axis=1)
-        live = jnp.concatenate([mask_ref[:, row, cols] for row in rows], axis=1)
-        if lon_total & (lon_total - 1):
-            node_row = lax.div(target, jnp.full_like(target, lon_total))
-        else:
-            node_row = lax.shift_right_logical(
-                target, jnp.full_like(target, lon_total.bit_length() - 1)
-            )
-        node_col = target - node_row * lon_total - lon_start + reach
-        node_col = jnp.where(node_col < 0, node_col + lon_total, node_col)
-        node_col = jnp.where(node_col >= lon_total, node_col - lon_total, node_col)
-        node_row = node_row - lat_start + reach - row_tile * TILE_MESH_ROWS
-        node_col = node_col - col_tile * wide
-        first = node_row * wide + node_col
-        slot = jnp.where(node_col < wide, first, first + (plan.side_keys - wide))
-        slot_ref[tile] = jnp.where(live > 0, slot, -1)
+        row, col = divmod(tile, plan.col_tiles)
+        rows = range(row * plan.tile_grid_rows, (row + 1) * plan.tile_grid_rows)
+        cols = slice(col * plan.tile_grid_cols, (col + 1) * plan.tile_grid_cols)
+        slot_ref[tile] = jnp.concatenate([slots[:, row, cols] for row in rows], axis=1)
 
 
 def attend_tiles(
@@ -289,11 +291,6 @@
     mesh_load.wait()
     pack = pack_matrix(plan)
     pack_ref[...] = mm(pack, own_feat[...]).astype(jnp.bfloat16)
-    edges_load.wait()
-    mask_load.wait()
-    fill_slots(
-        plan, lat * plan.mesh_rows, lon * plan.mesh_cols, edges_ref, mask_ref, slot_ref
-    )
     pl.semaphore_wait(barrier, len(exchanges))
     corner, lon_rim = plan.corner, plan.lon_rim
     sent = []
@@ -319,6 +316,11 @@
     for copy in above + beside:
         copy.start()
 
+    edges_load.wait()
+    mask_load.wait()
+    fill_slots(
+        plan, lat * plan.mesh_rows, lon * plan.mesh_cols, edges_ref, mask_ref, slot_ref
+    )
     grid_load.wait()
     wq_load.wait()
 

time: 45 us -> 44.7 us (level)
  no operation moved by 1% of the time
where the time goes in v6:
time: 44.7 us; the launch traced here: 44.6 us
  Pallas kernels  43.9 us (98%)
  between operations  0.64 us (1%)
    pallas_call x1, Pallas kernels, local(): pl.pallas_call(functools.partial(layer_kernel, plan), out_shape=(jax.Shap...  41.4 us
    pallas_call x1, Pallas kernels, local(): pl.pallas_call(functools.partial(store_kernel, own), out_shape=tuple((jax...  2.5 us

profile of v6, /device:TPU:0, one launch (start us, length us, event | category | flops | bytes accessed | tf_op | source)
XLA Modules:
  0.0 44.6 jit_solution(18368186249151582868)
XLA Ops:
  0.6 41.4 %shard_map.112 = (bf16[512,1024]{1,0:T(8,128)(2,1)}, bf16[512,1024]{1,0:T(8,128)(2,1)}, bf16[128,1024]{1,0:T(8,128)(2,1)}) custom-call(bf16[512,1024]{1,0:T(8,128)(2,1)} %bitcast.6, bf16[128,1024]{1,0:T(8,128)(2,1)} %bitcast.10, s32[12,16,32]{2,1,0:T(8,128)} %edges_in.1, s32[12,16,32]{2,1,0:T(8,128)} %mask_in.1, bf16[1024,1024]{1,0:T(8,128)(2,1)} %wq_in.1, ...), custom_call_target="tpu_custom_call" | custom-call | flops 7516192768 | bytes 12582912 | tf_op jit(solution)/shard_map/pallas_call | solution.py:504
  42.1 2.5 %shard_map.113 = (bf16[512,1024]{1,0:T(8,128)(2,1)}, bf16[512,1024]{1,0:T(8,128)(2,1)}, bf16[128,1024]{1,0:T(8,128)(2,1)}) custom-call(bf16[512,1024]{1,0:T(8,128)(2,1)} %get-tuple-element.9.refs_0_, bf16[512,1024]{1,0:T(8,128)(2,1)} %get-tuple-element.10.refs_1_, bf16[128,1024]{1,0:T(8,128)(2,1)} %get-tuple-element.11.refs_2_), custom_call_target="tpu_custom_call" | custom-call | tf_op jit(solution)/shard_map/pallas_call | solution.py:562

commit v7 on v6

--- a/solution.py
+++ b/solution.py
@@ -210,7 +210,7 @@
                 ref[window, lanes] += block[first : first + window.size]
 
         def first_products(index):
-            lanes = slice(index * pair, (index + 1) * pair)
+            lanes = pl.ds(pl.multiple_of(index * pair, pair), pair)
             q2 = split(points_of(q_ref, lanes))
             d2 = split(points_of(d_ref, lanes))
             k2 = window_of(k_ref, lanes)
@@ -230,11 +230,14 @@
             add_window(dk_ref, lanes, mm(d_score, q2))
             add_window(dv_ref, lanes, mm(half, d2))
 
-        ready = first_products(0)
-        for index in range(pairs):
-            following = first_products(index + 1) if index + 1 < pairs else None
-            rest(*ready)
-            ready = following
+        def two_pairs(index, inner):
+            first = first_products(2 * index)
+            second = first_products(2 * index + 1)
+            rest(*first)
+            rest(*second)
+            return inner
+
+        lax.fori_loop(0, pairs // 2, two_pairs, 0)
         return carry
 
     lax.fori_loop(0, plan.tiles, tile_step, 0)

time: 44.7 us -> 46.5 us (1.040)
  Pallas kernels: 43.9 us -> 45.7 us
    pallas_call x1, Pallas kernels: 41.4 us -> 43.2 us  [local(): pl.pallas_call(functools.partial(layer_kernel, plan), out_shape=(jax.Shap...]
where the time goes in v7:
time: 46.5 us; the launch traced here: 46.4 us
  Pallas kernels  45.7 us (98%)
  between operations  0.64 us (1%)
    pallas_call x1, Pallas kernels, local(): pl.pallas_call(functools.partial(layer_kernel, plan), out_shape=(jax.Shap...  43.2 us
    pallas_call x1, Pallas kernels, local(): pl.pallas_call(functools.partial(store_kernel, own), out_shape=tuple((jax...  2.5 us

profile of v7, /device:TPU:0, one launch (start us, length us, event | category | flops | bytes accessed | tf_op | source)
XLA Modules:
  0.0 46.4 jit_solution(9721181739759245479)
XLA Ops:
  0.6 43.2 %shard_map.112 = (bf16[512,1024]{1,0:T(8,128)(2,1)}, bf16[512,1024]{1,0:T(8,128)(2,1)}, bf16[128,1024]{1,0:T(8,128)(2,1)}) custom-call(bf16[512,1024]{1,0:T(8,128)(2,1)} %bitcast.6, bf16[128,1024]{1,0:T(8,128)(2,1)} %bitcast.10, s32[12,16,32]{2,1,0:T(8,128)} %edges_in.1, s32[12,16,32]{2,1,0:T(8,128)} %mask_in.1, bf16[1024,1024]{1,0:T(8,128)(2,1)} %wq_in.1, ...), custom_call_target="tpu_custom_call" | custom-call | flops 7516192768 | bytes 12582912 | tf_op jit(solution)/shard_map/pallas_call | solution.py:507
  43.9 2.5 %shard_map.113 = (bf16[512,1024]{1,0:T(8,128)(2,1)}, bf16[512,1024]{1,0:T(8,128)(2,1)}, bf16[128,1024]{1,0:T(8,128)(2,1)}) custom-call(bf16[512,1024]{1,0:T(8,128)(2,1)} %get-tuple-element.9.refs_0_, bf16[512,1024]{1,0:T(8,128)(2,1)} %get-tuple-element.10.refs_1_, bf16[128,1024]{1,0:T(8,128)(2,1)} %get-tuple-element.11.refs_2_), custom_call_target="tpu_custom_call" | custom-call | tf_op jit(solution)/shard_map/pallas_call | solution.py:565
